TPU v7x, 768 devices: a whole 4x8x12 slice. The times are simulated.
768 devices in a mesh: intra: 64 (over x, y, z_hi), inter: 12 (over z_lo, core).
Axes of the slice: x: 4, y: 8, z: 12 (z_hi: 2, z_lo: 6; z = z_hi * 6 + z_lo), core: 2. Of those that a mesh axis runs over, the one named last changes fastest.
Arguments:
- tokens: bfloat16 [320, 8192], P(None, 'intra'), may hold values from -6 to 6
- grad_out: bfloat16 [320, 8192], P(None, 'intra'), may hold values from -1 to 1
- up_codes: int32 [8192, 30720], P('intra', 'inter'), may hold values from -127 to 127
- up_scales: float32 [8192, 120], P('intra', 'inter'), may hold values from 6.629126e-05 to 0.0003314563
- down_codes: int32 [8192, 30720], P('intra', 'inter'), may hold values from -127 to 127
- down_scales: float32 [8192, 120], P('intra', 'inter'), may hold values from 6.629126e-05 to 0.0003314563
Outputs:
- grad_up: bfloat16 [8192, 30720], P('intra', 'inter')
- grad_down: bfloat16 [8192, 30720], P('intra', 'inter')
- grad_tokens: bfloat16 [320, 8192], P(None, 'intra')
All inputs are finite; a program needn't handle non-finite values.
Results may differ from a plain program's by a relative error of at most 0.007.
Values may be sent and summed in bfloat16 or wider, within the bound.
No kernel may reach another device: no remote copies, remote signals or barrier semaphores. Data moves between devices by JAX's collectives and lax.ppermute only.
A program may use at most 64 MiB of HBM per device.

v0:
```python
import math

import jax
import jax.numpy as jnp
from jax import lax
from jax.sharding import PartitionSpec as P

coef = math.sqrt(2.0 / math.pi)


def gelu_parts(pre):
    inner = coef * (pre + 0.044715 * pre * pre * pre)
    tanh_value = jnp.tanh(inner)
    value = 0.5 * pre * (1.0 + tanh_value)
    slope = 0.5 * (1.0 + tanh_value) + 0.5 * pre * (1.0 - tanh_value * tanh_value) * coef * (
        1.0 + 3.0 * 0.044715 * pre * pre
    )
    return (value, slope)


def dequantize(codes, scales):
    rows = codes.shape[0]
    units = codes.shape[1]
    shaped = codes.astype(jnp.float32).reshape(rows, units // 256, 256)
    return (shaped * scales[:, :, None]).reshape(rows, units).astype(jnp.bfloat16)


def shards(tokens, grad_out, up_codes, up_scales, down_codes, down_scales):
    w_up = dequantize(up_codes, up_scales)
    w_down = dequantize(down_codes, down_scales)
    contract = (((0,), (0,)), ((), ()))
    across = (((1,), (1,)), ((), ()))
    tok_part = tokens
    grad_part = grad_out
    first = jnp.dot(tok_part, w_up, preferred_element_type=jnp.float32)
    second = jnp.dot(grad_part, w_down, preferred_element_type=jnp.float32)
    share = lax.psum_scatter(
        jnp.concatenate([first, second], axis=1), "intra", scatter_dimension=0, tiled=True
    )
    half = share.shape[1] // 2
    value, slope = gelu_parts(share[:, :half])
    hidden_share = value.astype(jnp.bfloat16)
    dpre_share = (share[:, half:] * slope).astype(jnp.bfloat16)
    pieces = (
        lax.all_gather(hidden_share, "intra", axis=0, tiled=True),
        lax.all_gather(dpre_share, "intra", axis=0, tiled=True),
    )
    hidden_piece, dpre_piece = pieces
    tok_part = tokens
    grad_part = grad_out
    up_part = lax.dot_general(tok_part, dpre_piece, contract, preferred_element_type=jnp.float32)
    down_part = lax.dot_general(
        grad_part, hidden_piece, contract, preferred_element_type=jnp.float32
    )
    up_part, down_part = (up_part, down_part)
    input_piece = lax.dot_general(pieces[1], w_up, across, preferred_element_type=jnp.float32)
    grad_up = up_part
    grad_down = down_part
    input_sum = input_piece
    grad_up, grad_down, input_sum = (grad_up, grad_down, input_sum)
    summed = lax.psum(input_sum, "inter")
    return (
        grad_up.astype(jnp.bfloat16),
        grad_down.astype(jnp.bfloat16),
        summed.astype(jnp.bfloat16),
    )


def solution(mesh):
    in_specs = (
        P(None, "intra"),
        P(None, "intra"),
        P("intra", "inter"),
        P("intra", "inter"),
        P("intra", "inter"),
        P("intra", "inter"),
    )
    out_specs = (P("intra", "inter"), P("intra", "inter"), P(None, "intra"))
    return jax.shard_map(shards, mesh=mesh, in_specs=in_specs, out_specs=out_specs, check_vma=False)
```

profile of v0, /device:TPU:1, one launch (start us, length us, event | category | flops | bytes accessed | tf_op | source)
XLA Modules:
  0.0 1674.6 jit_solution(16233635755688323082)
XLA Ops:
  7.2 0.0 copy-start
  7.2 0.0 all-reduce.4.cloned.1.call-start
  7.2 1.7 copy.17
  8.9 0.0 copy-start.2
  9.0 1.7 copy.18
  10.7 0.1 fusion.3
  10.8 0.0 copy-done
  10.8 0.0 copy-start.3
  10.8 0.6 convolution_bitcast_fusion.1
  11.4 0.1 copy-done.3
  11.5 0.1 fusion.2
  11.7 0.8 copy-done.1
  12.4 0.6 convolution_bitcast_fusion
  13.0 3.3 pad_maximum_fusion
  16.3 0.0 all-reduce.4.cloned.1.call-update
  16.3 0.0 all-gather.5.cloned.1.call-start
  16.4 1.3 dynamic-slice
  18.3 1222.0 %all-reduce.4.cloned.1.call-done = f32[320,5120]{1,0:T(8,128)} async-done(((f32[320,5120]{1,0:T(8,128)}), f32[320,5120]{1,0:T(8,128)}) %all-reduce.4.cloned.1.call-update) | async-done | bytes 6553616
  1240.4 1.7 fusion.11
  1242.1 0.0 all-gather.5.cloned.1.call-update
  1242.1 0.0 all-gather.7.cloned.1.call-start
  1242.1 0.7 all-gather.7.cloned.1.call-update
  1242.8 255.7 %all-gather.5.cloned.1.call-done = bf16[64,5,2560]{2,1,0:T(8,128)(2,1)} async-done(((bf16[1,5,2560]{2,1,0:T(8,128)(2,1)}), bf16[64,5,2560]{2,1,0:T(8,128)(2,1)}) %all-gather.5.cloned.1.call-update) | async-done | bytes 1638416 | tf_op jit(solution)/shard_map/all_gather | solution.py:46
  1498.5 2.8 reshape.15
  1501.3 0.6 fusion.13
  1501.9 0.7 fusion
  1502.6 1.1 copy.19
  1503.7 55.8 %all-reduce.5 = bf16[320,128]{1,0:T(8,128)(2,1)} all-reduce(f32[320,128]{1,0:T(8,128)S(1)} %fusion.13), channel_id=1, replica_groups=mesh['intra'=64,'inter'=12] {'inter'}, use_global_device_ids=true, to_apply=%region_1.0 | all-reduce | flops 40960 | bytes 245760 | tf_op jit(solution)/shard_map/psum | solution.py:61
  1559.5 103.9 %all-gather.7.cloned.1.call-done = bf16[64,5,2560]{2,1,0:T(8,128)(2,1)} async-done(((bf16[1,5,2560]{2,1,0:T(8,128)(2,1)}), bf16[64,5,2560]{2,1,0:T(8,128)(2,1)}) %all-gather.7.cloned.1.call-update) | async-done | bytes 1638416 | tf_op jit(solution)/shard_map/all_gather | solution.py:45
  1663.4 2.8 reshape.17
  1666.2 0.7 fusion.1
  1667.0 1.1 copy.20
  (2 shorter events, 0.0 us)
Async XLA Ops:
  7.2 3.7 copy-start
  7.2 1233.2 %all-reduce.4.cloned.1.call-start = ((), (), s32[]{:S(2)}) async-start(), calls=%async_computation.2 | async-start | bytes 13107200
  8.9 1.7 copy-start.2
  10.8 0.7 copy-start.3
  11.5 0.9 copy-start.1
  16.3 1482.2 %all-gather.5.cloned.1.call-start = ((), (), s32[]{:S(2)}) async-start(), calls=%async_computation | async-start | bytes 2662400 | tf_op jit(solution)/shard_map/all_gather | solution.py:46
  1242.1 421.3 %all-gather.7.cloned.1.call-start = ((), (), s32[]{:S(2)}) async-start(), calls=%async_computation.1 | async-start | bytes 2662400 | tf_op jit(solution)/shard_map/all_gather | solution.py:45
Sparse Core Ops, SparseCore 0:
  16.5 1223.8 all-reduce.3
  1247.2 251.2 all-gather.4
  1505.3 158.0 all-gather.6
where the time goes:
time: 1680 us; the launch traced here: 1670 us
  waiting for transfers between devices  1580 us (94%)
  blocking collectives  55.8 us (3%)
    unnamed x4, waiting for transfers between devices  1220 us
    all_gather x1, waiting for transfers between devices, shards(): lax.all_gather(dpre_share, 'intra', axis=0, tiled=True)  256 us
    all_gather x1, waiting for transfers between devices, shards(): lax.all_gather(hidden_share, 'intra', axis=0, tiled=True)  104 us
    psum x1, blocking collectives, shards(): summed = lax.psum(input_sum, 'inter')  55.8 us
  transfers between devices with their start and end apart: 3, of which 3 were waited for; matrix products, arithmetic and copies ran while one was open for 0% of the time, Pallas kernels for 0%

commit v1 on v0

v1 whole, which is shorter than its diff:
```python
import functools
import math

import jax
import jax.numpy as jnp
from jax import lax
from jax.experimental import pallas as pl
from jax.experimental.pallas import tpu as pltpu
from jax.sharding import Mesh
from jax.sharding import PartitionSpec as P

coef = math.sqrt(2.0 / math.pi)
f32 = jnp.float32
bf16 = jnp.bfloat16
LANES = 128
SCALE_BLOCK = 256


def gelu_parts(pre):
    inner = coef * (pre + 0.044715 * pre * pre * pre)
    tanh_value = jnp.tanh(inner)
    value = 0.5 * pre * (1.0 + tanh_value)
    slope = 0.5 * (1.0 + tanh_value) + 0.5 * pre * (1.0 - tanh_value * tanh_value) * coef * (
        1.0 + 3.0 * 0.044715 * pre * pre
    )
    return (value, slope)


def call(kernel, out_shape, *args, name):
    vmem = pl.BlockSpec(memory_space=pltpu.VMEM)
    return pl.pallas_call(
        kernel,
        out_shape=out_shape,
        in_specs=[vmem] * len(args),
        out_specs=jax.tree.map(lambda _: vmem, out_shape),
        compiler_params=pltpu.CompilerParams(vmem_limit_bytes=48 * 1024 * 1024),
        name=name,
    )(*args)


def pack_kernel(nx, tok_ref, grad_ref, uc_ref, us_ref, dc_ref, ds_ref, out_ref):
    feats, units = uc_ref.shape
    tok = tok_ref.shape[0]
    blocks = units // nx // LANES
    for s, (codes, scales, acts) in enumerate(((uc_ref, us_ref, tok_ref), (dc_ref, ds_ref, grad_ref))):
        for x in range(nx):
            for k in range(blocks):
                at = (x * blocks + k) * LANES
                b = at // SCALE_BLOCK
                w = codes[:, at : at + LANES].astype(f32) * scales[:, b : b + 1]
                out_ref[2 * x + s, k * feats : (k + 1) * feats, :] = w.astype(bf16)
            out_ref[2 * x + s, blocks * feats :, :] = acts[...]


def forward_kernel(feats, got_ref, out_ref):
    srcs = got_ref.shape[0]
    blocks = out_ref.shape[1] // LANES
    for k in range(blocks):
        total = None
        for s in range(srcs):
            part = jnp.dot(
                got_ref[s, blocks * feats :, :],
                got_ref[s, k * feats : (k + 1) * feats, :],
                preferred_element_type=f32,
            )
            total = part if total is None else total + part
        out_ref[:, k * LANES : (k + 1) * LANES] = total.astype(bf16)


def sum_kernel(got_ref, keep_ref, send_ref):
    for s in range(2):
        total = got_ref[s].astype(f32)
        for h in range(1, got_ref.shape[0] // 2):
            total = total + got_ref[2 * h + s].astype(f32)
        keep_ref[s] = total
        send_ref[s] = total.astype(bf16)


def gelu_kernel(keep_ref, got_ref, out_ref):
    pre = keep_ref[0] + got_ref[0].astype(f32)
    back = keep_ref[1] + got_ref[1].astype(f32)
    value, slope = gelu_parts(pre)
    hidden = value.astype(bf16)
    dpre = (back * slope).astype(bf16)
    for h in range(out_ref.shape[0] // 2):
        out_ref[2 * h] = dpre
        out_ref[2 * h + 1] = hidden


def backward_kernel(feats, got_ref, act_ref, out_ref):
    srcs = got_ref.shape[0]
    blocks = act_ref.shape[1] // LANES
    act = act_ref[...]
    for s in range(srcs):
        acts = got_ref[s, blocks * feats :, :]
        grad = lax.dot_general(acts, act, (((0,), (0,)), ((), ())), preferred_element_type=f32)
        total = None
        for k in range(blocks):
            cols = slice(k * LANES, (k + 1) * LANES)
            out_ref[s, k * feats : (k + 1) * feats, :] = grad[:, cols].astype(bf16)
            part = lax.dot_general(
                act[:, cols],
                got_ref[s, k * feats : (k + 1) * feats, :],
                (((1,), (1,)), ((), ())),
                preferred_element_type=f32,
            )
            total = part if total is None else total + part
        out_ref[s, blocks * feats :, :] = total.astype(bf16)


def input_kernel(at, got_ref, out_ref):
    rows = got_ref.shape[1] - at
    total = got_ref[0, at:, :].astype(f32)
    for x in range(1, got_ref.shape[0] // 2):
        total = total + got_ref[2 * x, at:, :].astype(f32)
    out_ref[:rows, :] = total.astype(bf16)
    if out_ref.shape[0] > rows:
        out_ref[rows:, :] = jnp.zeros((out_ref.shape[0] - rows, LANES), bf16)


def unpack_kernel(feats, got_ref, up_ref, down_ref):
    nx = got_ref.shape[0] // 2
    blocks = up_ref.shape[1] // nx // LANES
    for s, out in enumerate((up_ref, down_ref)):
        for x in range(nx):
            for k in range(blocks):
                at = (x * blocks + k) * LANES
                out[:, at : at + LANES] = got_ref[2 * x + s, k * feats : (k + 1) * feats, :]


def reduce_kernel(got_ref, out_ref):
    total = got_ref[0].astype(f32)
    for i in range(1, got_ref.shape[0]):
        total = total + got_ref[i].astype(f32)
    final = total.astype(bf16)
    for i in range(out_ref.shape[0]):
        out_ref[i] = final


def exchange(value, axes):
    return lax.all_to_all(value, axes, 0, 0, tiled=True)


def shards(sizes, tokens, grad_out, up_codes, up_scales, down_codes, down_scales):
    nx, nyh, nyl, nzl, ncore = (sizes[a] for a in ("x", "yh", "yl", "zl", "core"))
    feats, units = up_codes.shape
    tok = tokens.shape[0]
    mine = units // nx
    srcs = nx * nyl
    share = tok // (nyh * nyl)
    rows = feats * (mine // LANES)
    S = jax.ShapeDtypeStruct

    packed = call(
        functools.partial(pack_kernel, nx),
        S((srcs, rows + tok, LANES), bf16),
        tokens, grad_out, up_codes, up_scales, down_codes, down_scales,
        name="pack",
    )
    got = exchange(packed, ("x", "yl"))
    part = call(functools.partial(forward_kernel, feats), S((tok, mine), bf16), got, name="forward")
    terms = exchange(part.reshape(nyh * nyl, share, mine), ("yh", "yl"))
    keep, send = call(
        sum_kernel, (S((2, share, mine), f32), S((2, share, mine), bf16)), terms, name="sum"
    )
    other = lax.ppermute(send, "zh", [(0, 1), (1, 0)])
    acts = call(gelu_kernel, S((nyh * nyl, share, mine), bf16), keep, other, name="gelu")
    act = exchange(acts, ("yh", "yl")).reshape(tok, mine)
    grads = call(
        functools.partial(backward_kernel, feats), S((srcs, rows + tok, LANES), bf16), got, act, name="backward"
    )
    home = exchange(grads, ("x", "yl"))
    inter = nzl * ncore
    slab = -(-tok // (16 * inter)) * 16
    padded = call(functools.partial(input_kernel, rows), S((inter * slab, LANES), bf16), home, name="input")
    slabs = exchange(padded.reshape(inter, slab, LANES), ("zl", "core"))
    final = call(reduce_kernel, S((inter, slab, LANES), bf16), slabs, name="reduce")
    grad_tokens = exchange(final, ("zl", "core")).reshape(inter * slab, LANES)[:tok]
    grad_up, grad_down = call(
        functools.partial(unpack_kernel, feats),
        (S((feats, units), bf16), S((feats, units), bf16)),
        home,
        name="unpack",
    )
    return grad_up, grad_down, grad_tokens


AXES = ("x", "yh", "yl", "zh", "zl", "core")
SIZES = (4, 4, 2, 2, 6, 2)


def solution(mesh, sizes=SIZES):
    fine = Mesh(mesh.devices.reshape(sizes), AXES)
    intra, inter = AXES[:4], AXES[4:]
    in_specs = (
        P(None, intra),
        P(None, intra),
        P(intra, inter),
        P(intra, inter),
        P(intra, inter),
        P(intra, inter),
    )
    out_specs = (P(intra, inter), P(intra, inter), P(None, intra))
    return jax.shard_map(
        functools.partial(shards, dict(zip(AXES, sizes))),
        mesh=fine,
        in_specs=in_specs,
        out_specs=out_specs,
        check_vma=False,
    )
```

time: 1680 us -> 158 us (0.09)
  waiting for transfers between devices: 1580 us -> 10.1 us
  blocking collectives: 55.8 us -> 115 us
  starting transfers between devices: 0.12 us -> 18.5 us
    unnamed x4 -> x0, waiting for transfers between devices: 1220 us -> none
    all_gather x2 -> x0, waiting for transfers between devices: 360 us -> none  [the longest x1 256 us: shards(): lax.all_gather(dpre_share, 'intra', axis=0, tiled=True)]
    all_to_all x0 -> x5, blocking collectives: none -> 115 us  [exchange(): return lax.all_to_all(value, axes, 0, 0, tiled=True)]
    psum x1 -> x0, blocking collectives: 55.8 us -> none  [shards(): summed = lax.psum(input_sum, 'inter')]
  transfers between devices with their start and end apart: 3 -> 2, of which waited for: 3 -> 2; matrix products, arithmetic and copies ran while one was open for 0% -> 0% of each run, Pallas kernels for 0% -> 1%
where the time goes in v1:
time: 158 us; the launch traced here: 157 us
  blocking collectives  115 us (73%)
  starting transfers between devices  18.5 us (12%)
  waiting for transfers between devices  10.1 us (6%)
  local copies, waits for them, and re-layouts  6.64 us (4%)
  Pallas kernels  5.81 us (4%)
    all_to_all x5, blocking collectives, exchange(): return lax.all_to_all(value, axes, 0, 0, tiled=True)  115 us
    ppermute x1, starting transfers between devices, shards(): other = lax.ppermute(send, 'zh', [(0, 1), (1, 0)])  14.9 us
    all_to_all x1, waiting for transfers between devices, exchange(): return lax.all_to_all(value, axes, 0, 0, tiled=True)  7.9 us
    unnamed x10, local copies, waits for them, and re-layouts  6 us
    pallas_call x8, Pallas kernels, call(): pl.pallas_call(kernel, out_shape=out_shape, in_specs=[vmem] * len(args),...  5.81 us
    all_to_all x1, starting transfers between devices, exchange(): return lax.all_to_all(value, axes, 0, 0, tiled=True)  3.66 us
  transfers between devices with their start and end apart: 2, of which 2 were waited for; matrix products, arithmetic and copies ran while one was open for 0% of the time, Pallas kernels for 1%

profile of v1, /device:TPU:1, one launch (start us, length us, event | category | flops | bytes accessed | tf_op | source)
XLA Modules:
  0.0 157.1 jit_solution(12750836738748089530)
XLA Ops:
  0.6 0.8 copy.9.us_ref
  1.4 0.8 copy.10.ds_ref
  2.2 0.0 copy-start
  2.2 1.3 copy-done
  3.5 0.0 copy-start.1
  3.6 1.3 copy-done.1
  4.9 0.0 copy-start.2
  4.9 0.9 copy-done.2
  5.8 0.0 copy-start.3
  5.8 0.9 copy-done.3
  6.6 0.8 pack.1
  7.5 23.9 %all_to_all.30.got_ref = bf16[8,960,128]{2,1,0:T(8,128)(2,1)S(1)} all-to-all(bf16[8,960,128]{2,1,0:T(8,128)(2,1)S(1)} %pack.1), channel_id=1, replica_groups=mesh['x'=4,'yh'=4,'yl'=2,'zh'=2,'zl'=6,'core'=2] {'x','yl'}, dimensions={0} | all-to-all | bytes 3932160 | tf_op jit(solution)/shard_map/all_to_all | solution.py:141
  31.4 1.0 forward.1
  32.4 24.3 %all_to_all.31.got_ref = bf16[8,40,640]{2,1,0:T(8,128)(2,1)S(1)} all-to-all(bf16[8,40,640]{2,1,0:T(8,128)(2,1)S(1)} %bitcast.5), channel_id=1, replica_groups=mesh['x'=4,'yh'=4,'yl'=2,'zh'=2,'zl'=6,'core'=2] {'yh','yl'}, dimensions={0} | all-to-all | bytes 819200 | tf_op jit(solution)/shard_map/all_to_all | solution.py:141
  56.7 0.1 sum.1
  56.7 14.9 %collective-permute-start = (bf16[2,40,640]{2,1,0:T(8,128)(2,1)S(1)}, bf16[2,40,640]{2,1,0:T(8,128)(2,1)S(1)}, u32[]{:S(2)}, u32[]{:S(2)}) collective-permute-start(bf16[2,40,640]{2,1,0:T(8,128)(2,1)S(1)} %get-tuple-element.8), channel_id=1, source_target_pairs={{0,12},{12,0},{1,13},{13,1},{2,14},{14,2},{3,15},{15,3},{4,16},{16... | collective-permute-start | bytes 307208 | tf_op jit(solution)/shard_map/ppermute | solution.py:166
  71.6 2.2 %collective-permute-done.got_ref = bf16[2,40,640]{2,1,0:T(8,128)(2,1)S(1)} collective-permute-done((bf16[2,40,640]{2,1,0:T(8,128)(2,1)S(1)}, bf16[2,40,640]{2,1,0:T(8,128)(2,1)S(1)}, u32[]{:S(2)}, u32[]{:S(2)}) %collective-permute-start) | collective-permute-done | bytes 102432 | tf_op jit(solution)/shard_map/ppermute | solution.py:166
  73.8 0.1 gelu.1
  74.0 14.9 %all_to_all.32 = bf16[8,40,640]{2,1,0:T(8,128)(2,1)S(1)} all-to-all(bf16[8,40,640]{2,1,0:T(8,128)(2,1)S(1)} %gelu.1), channel_id=1, replica_groups=mesh['x'=4,'yh'=4,'yl'=2,'zh'=2,'zl'=6,'core'=2] {'yh','yl'}, dimensions={0} | all-to-all | bytes 819200 | tf_op jit(solution)/shard_map/all_to_all | solution.py:141
  88.9 1.9 %backward.1 = bf16[8,960,128]{2,1,0:T(8,128)(2,1)S(1)} custom-call(bf16[8,960,128]{2,1,0:T(8,128)(2,1)S(1)} %all_to_all.30.got_ref, bf16[320,640]{1,0:T(8,128)(2,1)S(1)} %bitcast.4), custom_call_target="tpu_custom_call" | custom-call | tf_op jit(solution)/shard_map/backward/pallas_call | solution.py:31
  90.7 21.9 %all_to_all.33.got_ref = bf16[8,960,128]{2,1,0:T(8,128)(2,1)S(1)} all-to-all(bf16[8,960,128]{2,1,0:T(8,128)(2,1)S(1)} %backward.1), channel_id=1, replica_groups=mesh['x'=4,'yh'=4,'yl'=2,'zh'=2,'zl'=6,'core'=2] {'x','yl'}, dimensions={0} | all-to-all | bytes 3932160 | tf_op jit(solution)/shard_map/all_to_all | solution.py:141
  112.7 30.3 %all_to_all.34.got_ref = bf16[12,32,128]{2,1,0:T(8,128)(2,1)S(1)} all-to-all(bf16[12,32,128]{2,1,0:T(8,128)(2,1)S(1)} %bitcast.6), channel_id=1, replica_groups=mesh['x'=4,'yh'=4,'yl'=2,'zh'=2,'zl'=6,'core'=2] {'zl','core'}, dimensions={0} | all-to-all | bytes 196608 | tf_op jit(solution)/shard_map/all_to_all | solution.py:141
  143.0 0.7 reduce.1
  143.6 3.7 %all-to-all-start.5 = ((bf16[12,32,128]{2,1,0:T(8,128)(2,1)}), bf16[12,32,128]{2,1,0:T(8,128)(2,1)S(1)}, u32[]{:S(2)}, u32[]{:S(2)}) async-start(bf16[12,32,128]{2,1,0:T(8,128)(2,1)} %reduce.1), calls=%async_computation.5 | async-start | bytes 196608 | tf_op jit(solution)/shard_map/all_to_all | solution.py:141
  147.3 1.3 unpack.1
  148.6 7.9 %all-to-all-done.5 = bf16[12,32,128]{2,1,0:T(8,128)(2,1)S(1)} async-done(((bf16[12,32,128]{2,1,0:T(8,128)(2,1)}), bf16[12,32,128]{2,1,0:T(8,128)(2,1)S(1)}, u32[]{:S(2)}, u32[]{:S(2)}) %all-to-all-start.5) | async-done | bytes 98336 | tf_op jit(solution)/shard_map/all_to_all | solution.py:141
  156.5 0.6 slice.8
  (1 shorter events, 0.0 us)
Async XLA Ops:
  2.2 1.3 copy-start
  3.5 1.3 copy-start.1
  4.9 0.9 copy-start.2
  5.8 0.9 copy-start.3
  56.7 17.1 %collective-permute-start = (bf16[2,40,640]{2,1,0:T(8,128)(2,1)S(1)}, bf16[2,40,640]{2,1,0:T(8,128)(2,1)S(1)}, u32[]{:S(2)}, u32[]{:S(2)}) collective-permute-start(bf16[2,40,640]{2,1,0:T(8,128)(2,1)S(1)} %get-tuple-element.8), channel_id=1, source_target_pairs={{0,12},{12,0},{1,13},{13,1},{2,14},{14,2},{3,15},{15,3},{4,16},{16... | collective-permute-start | bytes 307208 | tf_op jit(solution)/shard_map/ppermute | solution.py:166
  143.6 12.8 %all-to-all-start.5 = ((bf16[12,32,128]{2,1,0:T(8,128)(2,1)}), bf16[12,32,128]{2,1,0:T(8,128)(2,1)S(1)}, u32[]{:S(2)}, u32[]{:S(2)}) async-start(bf16[12,32,128]{2,1,0:T(8,128)(2,1)} %reduce.1), calls=%async_computation.5 | async-start | bytes 196608 | tf_op jit(solution)/shard_map/all_to_all | solution.py:141

commit v2 on v1

--- a/solution.py
+++ b/solution.py
@@ -38,18 +38,69 @@
     )(*args)
 
 
-def pack_kernel(nx, tok_ref, grad_ref, uc_ref, us_ref, dc_ref, ds_ref, out_ref):
+def pack_kernel(nx, tok_ref, grad_ref, uc_ref, us_ref, dc_ref, ds_ref, out_ref, codes, scales, sems, act_sems):
     feats, units = uc_ref.shape
-    tok = tok_ref.shape[0]
-    blocks = units // nx // LANES
-    for s, (codes, scales, acts) in enumerate(((uc_ref, us_ref, tok_ref), (dc_ref, ds_ref, grad_ref))):
-        for x in range(nx):
+    width = units // nx
+    blocks = width // LANES
+    sides = ((uc_ref, us_ref, tok_ref), (dc_ref, ds_ref, grad_ref))
+    scale_copies = [
+        pltpu.make_async_copy(side[1], scales.at[s], sems.at[s, nx]) for s, side in enumerate(sides)
+    ]
+    for copy in scale_copies:
+        copy.start()
+    code_copies = {}
+    for x in range(nx):
+        for s, side in enumerate(sides):
+            cols = pl.ds(x * width, width)
+            code_copies[s, x] = pltpu.make_async_copy(
+                side[0].at[:, cols], codes.at[s, :, cols], sems.at[s, x]
+            )
+            code_copies[s, x].start()
+    act_copies = []
+    for x in range(nx):
+        for s, side in enumerate(sides):
+            act_copies.append(
+                pltpu.make_async_copy(
+                    side[2],
+                    out_ref.at[2 * x + s, pl.ds(blocks * feats, tok_ref.shape[0]), :],
+                    act_sems.at[2 * x + s],
+                )
+            )
+            act_copies[-1].start()
+    columns = []
+    for s in range(2):
+        scale_copies[s].wait()
+        columns.append(scales[s].T)
+    for x in range(nx):
+        for s in range(2):
+            code_copies[s, x].wait()
             for k in range(blocks):
                 at = (x * blocks + k) * LANES
                 b = at // SCALE_BLOCK
-                w = codes[:, at : at + LANES].astype(f32) * scales[:, b : b + 1]
+                w = codes[s, :, at : at + LANES].astype(f32) * columns[s][:, b : b + 1]
                 out_ref[2 * x + s, k * feats : (k + 1) * feats, :] = w.astype(bf16)
-            out_ref[2 * x + s, blocks * feats :, :] = acts[...]
+    for copy in act_copies:
+        copy.wait()
+
+
+def pack(nx, tokens, grad_out, up_codes, up_scales, down_codes, down_scales):
+    feats, units = up_codes.shape
+    tok = tokens.shape[0]
+    rows = feats * (units // nx // LANES)
+    return pl.pallas_call(
+        functools.partial(pack_kernel, nx),
+        out_shape=jax.ShapeDtypeStruct((2 * nx, rows + tok, LANES), bf16),
+        in_specs=[pl.BlockSpec(memory_space=pltpu.HBM)] * 6,
+        out_specs=pl.BlockSpec(memory_space=pltpu.VMEM),
+        scratch_shapes=[
+            pltpu.VMEM((2, feats, units), jnp.int32),
+            pltpu.VMEM((2, units // SCALE_BLOCK, feats), f32),
+            pltpu.SemaphoreType.DMA((2, nx + 1)),
+            pltpu.SemaphoreType.DMA((2 * nx,)),
+        ],
+        compiler_params=pltpu.CompilerParams(vmem_limit_bytes=56 * 1024 * 1024),
+        name="pack",
+    )(tokens, grad_out, up_codes, up_scales.T, down_codes, down_scales.T)
 
 
 def forward_kernel(feats, got_ref, out_ref):
@@ -87,35 +138,50 @@
         out_ref[2 * h + 1] = hidden
 
 
-def backward_kernel(feats, got_ref, act_ref, out_ref):
-    srcs = got_ref.shape[0]
+def terms_kernel(feats, got_ref, act_ref, out_ref):
     blocks = act_ref.shape[1] // LANES
     act = act_ref[...]
-    for s in range(srcs):
-        acts = got_ref[s, blocks * feats :, :]
-        grad = lax.dot_general(acts, act, (((0,), (0,)), ((), ())), preferred_element_type=f32)
+    for s in range(got_ref.shape[0]):
         total = None
         for k in range(blocks):
-            cols = slice(k * LANES, (k + 1) * LANES)
-            out_ref[s, k * feats : (k + 1) * feats, :] = grad[:, cols].astype(bf16)
             part = lax.dot_general(
-                act[:, cols],
+                act[:, k * LANES : (k + 1) * LANES],
                 got_ref[s, k * feats : (k + 1) * feats, :],
                 (((1,), (1,)), ((), ())),
                 preferred_element_type=f32,
             )
             total = part if total is None else total + part
-        out_ref[s, blocks * feats :, :] = total.astype(bf16)
-
-
-def input_kernel(at, got_ref, out_ref):
-    rows = got_ref.shape[1] - at
-    total = got_ref[0, at:, :].astype(f32)
+        out_ref[s] = total.astype(bf16)
+
+
+def grads_kernel(feats, got_ref, act_ref, out_ref):
+    blocks = act_ref.shape[1] // LANES
+    act = act_ref[...]
+    for s in range(got_ref.shape[0]):
+        acts = got_ref[s, blocks * feats :, :]
+        grad = lax.dot_general(acts, act, (((0,), (0,)), ((), ())), preferred_element_type=f32)
+        for k in range(blocks):
+            out_ref[s, k * feats : (k + 1) * feats, :] = grad[:, k * LANES : (k + 1) * LANES].astype(bf16)
+
+
+def home_kernel(got_ref, out_ref):
+    total = got_ref[0].astype(f32)
     for x in range(1, got_ref.shape[0] // 2):
-        total = total + got_ref[2 * x, at:, :].astype(f32)
-    out_ref[:rows, :] = total.astype(bf16)
-    if out_ref.shape[0] > rows:
-        out_ref[rows:, :] = jnp.zeros((out_ref.shape[0] - rows, LANES), bf16)
+        total = total + got_ref[2 * x].astype(f32)
+    out_ref[...] = total
+
+
+def pair_kernel(a_ref, b_ref, out_ref):
+    out_ref[...] = (a_ref[...] + b_ref[...]).astype(out_ref.dtype)
+
+
+def triple_kernel(own_ref, prev_ref, next_ref, out_ref):
+    pos = lax.div(lax.axis_index("zl"), 2)
+    own, prev, nxt = (r[...].astype(f32) for r in (own_ref, prev_ref, next_ref))
+    first = jnp.where(pos == 0, own, jnp.where(pos == 1, prev, nxt))
+    second = jnp.where(pos == 1, own, jnp.where(pos == 2, prev, nxt))
+    third = jnp.where(pos == 2, own, jnp.where(pos == 0, prev, nxt))
+    out_ref[...] = (first + second + third).astype(bf16)
 
 
 def unpack_kernel(feats, got_ref, up_ref, down_ref):
@@ -128,17 +194,19 @@
                 out[:, at : at + LANES] = got_ref[2 * x + s, k * feats : (k + 1) * feats, :]
 
 
-def reduce_kernel(got_ref, out_ref):
-    total = got_ref[0].astype(f32)
-    for i in range(1, got_ref.shape[0]):
-        total = total + got_ref[i].astype(f32)
-    final = total.astype(bf16)
-    for i in range(out_ref.shape[0]):
-        out_ref[i] = final
-
-
 def exchange(value, axes):
     return lax.all_to_all(value, axes, 0, 0, tiled=True)
+
+
+def inter_sum(nzl, ncore, term):
+    S = jax.ShapeDtypeStruct
+    other = lax.ppermute(term, "core", [(i, i ^ 1) for i in range(ncore)])
+    term = call(pair_kernel, S(term.shape, f32), term, other, name="cores")
+    other = lax.ppermute(term, "zl", [(i, i ^ 1) for i in range(nzl)])
+    term = call(pair_kernel, S(term.shape, bf16), term, other, name="pairs")
+    prev = lax.ppermute(term, "zl", [(i, (i + 2) % nzl) for i in range(nzl)])
+    nxt = lax.ppermute(term, "zl", [(i, (i - 2) % nzl) for i in range(nzl)])
+    return call(triple_kernel, S(term.shape, bf16), term, prev, nxt, name="triples")
 
 
 def shards(sizes, tokens, grad_out, up_codes, up_scales, down_codes, down_scales):
@@ -151,12 +219,7 @@
     rows = feats * (mine // LANES)
     S = jax.ShapeDtypeStruct
 
-    packed = call(
-        functools.partial(pack_kernel, nx),
-        S((srcs, rows + tok, LANES), bf16),
-        tokens, grad_out, up_codes, up_scales, down_codes, down_scales,
-        name="pack",
-    )
+    packed = pack(nx, tokens, grad_out, up_codes, up_scales, down_codes, down_scales)
     got = exchange(packed, ("x", "yl"))
     part = call(functools.partial(forward_kernel, feats), S((tok, mine), bf16), got, name="forward")
     terms = exchange(part.reshape(nyh * nyl, share, mine), ("yh", "yl"))
@@ -166,16 +229,11 @@
     other = lax.ppermute(send, "zh", [(0, 1), (1, 0)])
     acts = call(gelu_kernel, S((nyh * nyl, share, mine), bf16), keep, other, name="gelu")
     act = exchange(acts, ("yh", "yl")).reshape(tok, mine)
-    grads = call(
-        functools.partial(backward_kernel, feats), S((srcs, rows + tok, LANES), bf16), got, act, name="backward"
-    )
+    terms = call(functools.partial(terms_kernel, feats), S((srcs, tok, feats), bf16), got, act, name="terms")
+    terms = exchange(terms, ("x", "yl"))
+    grads = call(functools.partial(grads_kernel, feats), S((srcs, rows, LANES), bf16), got, act, name="grads")
     home = exchange(grads, ("x", "yl"))
-    inter = nzl * ncore
-    slab = -(-tok // (16 * inter)) * 16
-    padded = call(functools.partial(input_kernel, rows), S((inter * slab, LANES), bf16), home, name="input")
-    slabs = exchange(padded.reshape(inter, slab, LANES), ("zl", "core"))
-    final = call(reduce_kernel, S((inter, slab, LANES), bf16), slabs, name="reduce")
-    grad_tokens = exchange(final, ("zl", "core")).reshape(inter * slab, LANES)[:tok]
+    grad_tokens = inter_sum(nzl, ncore, call(home_kernel, S((tok, feats), f32), terms, name="home"))
     grad_up, grad_down = call(
         functools.partial(unpack_kernel, feats),
         (S((feats, units), bf16), S((feats, units), bf16)),

time: 158 us -> 143 us (0.905)
  blocking collectives: 115 us -> 63.3 us
  starting transfers between devices: 18.5 us -> 47.5 us
  waiting for transfers between devices: 10.1 us -> 19.8 us
  local copies, waits for them, and re-layouts: 6.64 us -> 0.83 us
  Pallas kernels: 5.81 us -> 9.8 us
    all_to_all x5 -> x3, blocking collectives: 115 us -> 63.3 us  [exchange(): return lax.all_to_all(value, axes, 0, 0, tiled=True)]
    ppermute x0 -> x4, starting transfers between devices: none -> 25.5 us  [the longest x1 9.14 us: inter_sum(): other = lax.ppermute(term, 'core', [(i, i ^ 1) for i in range(ncore)])]
    ppermute x0 -> x4, waiting for transfers between devices: none -> 11.5 us  [the longest x1 4.26 us: inter_sum(): other = lax.ppermute(term, 'zl', [(i, i ^ 1) for i in range(nzl)])]
    unnamed x10 -> x2, local copies, waits for them, and re-layouts: 6 us -> 0.83 us
    pallas_call x0 -> x1, Pallas kernels: none -> 3.46 us  [pack(): pl.pallas_call(functools.partial(pack_kernel, nx), out_shape=jax.ShapeDty...]
    all_to_all x1 -> x2, starting transfers between devices: 3.66 us -> 7.11 us  [exchange(): return lax.all_to_all(value, axes, 0, 0, tiled=True)]
    all_to_all x1 -> x2, waiting for transfers between devices: 7.9 us -> 6.05 us  [exchange(): return lax.all_to_all(value, axes, 0, 0, tiled=True)]
    pallas_call x8 -> x10, Pallas kernels: 5.81 us -> 6.34 us  [call(): pl.pallas_call(kernel, out_shape=out_shape, in_specs=[vmem] * len(args),...]
  transfers between devices with their start and end apart: 2 -> 7, of which waited for: 2 -> 6; matrix products, arithmetic and copies ran while one was open for 0% -> 0% of each run, Pallas kernels for 1% -> 2%
where the time goes in v2:
time: 143 us; the launch traced here: 142 us
  blocking collectives  63.3 us (44%)
  starting transfers between devices  47.5 us (33%)
  waiting for transfers between devices  19.8 us (14%)
  Pallas kernels  9.8 us (7%)
    all_to_all x3, blocking collectives, exchange(): return lax.all_to_all(value, axes, 0, 0, tiled=True)  63.3 us
    ppermute x1, starting transfers between devices, shards(): other = lax.ppermute(send, 'zh', [(0, 1), (1, 0)])  14.9 us
    ppermute x1, starting transfers between devices, inter_sum(): other = lax.ppermute(term, 'core', [(i, i ^ 1) for i in range(ncore)])  9.14 us
    ppermute x1, starting transfers between devices, inter_sum(): nxt = lax.ppermute(term, 'zl', [(i, (i - 2) % nzl) for i in range(nzl)])  8.48 us
    all_to_all x2, starting transfers between devices, exchange(): return lax.all_to_all(value, axes, 0, 0, tiled=True)  7.11 us
    pallas_call x10, Pallas kernels, call(): pl.pallas_call(kernel, out_shape=out_shape, in_specs=[vmem] * len(args),...  6.34 us
    all_to_all x2, waiting for transfers between devices, exchange(): return lax.all_to_all(value, axes, 0, 0, tiled=True)  6.05 us
    ppermute x1, waiting for transfers between devices, inter_sum(): other = lax.ppermute(term, 'zl', [(i, i ^ 1) for i in range(nzl)])  4.26 us
  transfers between devices with their start and end apart: 7, of which 6 were waited for; matrix products, arithmetic and copies ran while one was open for 0% of the time, Pallas kernels for 2%

profile of v2, /device:TPU:1, one launch (start us, length us, event | category | flops | bytes accessed | tf_op | source)
XLA Modules:
  0.0 142.0 jit_solution(12746931584674054687)
XLA Ops:
  0.6 3.5 %pack.1 = bf16[8,960,128]{2,1,0:T(8,128)(2,1)} custom-call(bf16[320,128]{1,0:T(8,128)(2,1)} %tok_ref.1, bf16[320,128]{1,0:T(8,128)(2,1)} %grad_ref.1, s32[128,2560]{1,0:T(8,128)} %uc_ref.1, f32[10,128]{1,0:T(8,128)} %bitcast.7, s32[128,2560]{1,0:T(8,128)} %dc_ref.1, f32[10,128]{1,0:T(8,128)} %bitcast.8), custom_call_target="tpu_custom_call" | custom-call | tf_op jit(solution)/shard_map/pack/pallas_call | solution.py:90
  4.1 23.3 %all_to_all.25.got_ref = bf16[8,960,128]{2,1,0:T(8,128)(2,1)S(1)} all-to-all(bf16[8,960,128]{2,1,0:T(8,128)(2,1)} %pack.1), channel_id=1, replica_groups=mesh['x'=4,'yh'=4,'yl'=2,'zh'=2,'zl'=6,'core'=2] {'x','yl'}, dimensions={0} | all-to-all | bytes 3932160 | tf_op jit(solution)/shard_map/all_to_all | solution.py:198
  27.4 1.0 forward.1
  28.4 25.2 %all_to_all.26.got_ref = bf16[8,40,640]{2,1,0:T(8,128)(2,1)S(1)} all-to-all(bf16[8,40,640]{2,1,0:T(8,128)(2,1)S(1)} %bitcast.6), channel_id=1, replica_groups=mesh['x'=4,'yh'=4,'yl'=2,'zh'=2,'zl'=6,'core'=2] {'yh','yl'}, dimensions={0} | all-to-all | bytes 819200 | tf_op jit(solution)/shard_map/all_to_all | solution.py:198
  53.5 0.1 sum.1
  53.6 14.9 %collective-permute-start = (bf16[2,40,640]{2,1,0:T(8,128)(2,1)S(1)}, bf16[2,40,640]{2,1,0:T(8,128)(2,1)S(1)}, u32[]{:S(2)}, u32[]{:S(2)}) collective-permute-start(bf16[2,40,640]{2,1,0:T(8,128)(2,1)S(1)} %get-tuple-element.8), channel_id=1, source_target_pairs={{0,12},{12,0},{1,13},{13,1},{2,14},{14,2},{3,15},{15,3},{4,16},{16... | collective-permute-start | bytes 307208 | tf_op jit(solution)/shard_map/ppermute | solution.py:229
  68.5 2.2 %collective-permute-done.got_ref = bf16[2,40,640]{2,1,0:T(8,128)(2,1)S(1)} collective-permute-done((bf16[2,40,640]{2,1,0:T(8,128)(2,1)S(1)}, bf16[2,40,640]{2,1,0:T(8,128)(2,1)S(1)}, u32[]{:S(2)}, u32[]{:S(2)}) %collective-permute-start) | collective-permute-done | bytes 102432 | tf_op jit(solution)/shard_map/ppermute | solution.py:229
  70.7 0.1 gelu.1
  70.8 14.9 %all_to_all.27 = bf16[8,40,640]{2,1,0:T(8,128)(2,1)S(1)} all-to-all(bf16[8,40,640]{2,1,0:T(8,128)(2,1)S(1)} %gelu.1), channel_id=1, replica_groups=mesh['x'=4,'yh'=4,'yl'=2,'zh'=2,'zl'=6,'core'=2] {'yh','yl'}, dimensions={0} | all-to-all | bytes 819200 | tf_op jit(solution)/shard_map/all_to_all | solution.py:198
  85.7 1.0 terms.1
  86.7 0.0 copy-start
  86.7 0.8 copy-done
  87.6 3.5 %all-to-all-start.4 = ((bf16[8,320,128]{2,1,0:T(8,128)(2,1)}), bf16[8,320,128]{2,1,0:T(8,128)(2,1)S(1)}, u32[]{:S(2)}, u32[]{:S(2)}) async-start(bf16[8,320,128]{2,1,0:T(8,128)(2,1)} %copy-done), calls=%async_computation.4 | async-start | bytes 1310720 | tf_op jit(solution)/shard_map/all_to_all | solution.py:198
  91.1 2.1 %grads.1 = bf16[8,640,128]{2,1,0:T(8,128)(2,1)} custom-call(bf16[8,960,128]{2,1,0:T(8,128)(2,1)S(1)} %all_to_all.25.got_ref, bf16[320,640]{1,0:T(8,128)(2,1)S(1)} %bitcast.5), custom_call_target="tpu_custom_call" | custom-call | tf_op jit(solution)/shard_map/grads/pallas_call | solution.py:31
  93.2 6.1 %all-to-all-done.4.got_ref = bf16[8,320,128]{2,1,0:T(8,128)(2,1)S(1)} async-done(((bf16[8,320,128]{2,1,0:T(8,128)(2,1)}), bf16[8,320,128]{2,1,0:T(8,128)(2,1)S(1)}, u32[]{:S(2)}, u32[]{:S(2)}) %all-to-all-start.4) | async-done | bytes 655392 | tf_op jit(solution)/shard_map/all_to_all | solution.py:198
  99.3 3.6 %all-to-all-start.3 = ((bf16[8,640,128]{2,1,0:T(8,128)(2,1)}), bf16[8,640,128]{2,1,0:T(8,128)(2,1)S(1)}, u32[]{:S(2)}, u32[]{:S(2)}) async-start(bf16[8,640,128]{2,1,0:T(8,128)(2,1)} %grads.1), calls=%async_computation.3 | async-start | bytes 2621440 | tf_op jit(solution)/shard_map/all_to_all | solution.py:198
  102.9 9.1 %collective-permute-start.1 = (f32[320,128]{1,0:T(8,128)S(1)}, f32[320,128]{1,0:T(8,128)S(1)}, u32[]{:S(2)}, u32[]{:S(2)}) collective-permute-start(f32[320,128]{1,0:T(8,128)S(1)} %home.1.a_ref), channel_id=1, source_target_pairs={{0,1},{1,0},{2,3},{3,2},{4,5},{5,4},{6,7},{7,6},{8,9},{9,8},{10,11... | collective-permute-start | bytes 491528 | tf_op jit(solution)/shard_map/ppermute | solution.py:203
  112.1 1.0 collective-permute-done.1.b_ref
  113.1 3.7 %collective-permute-start.2 = (f32[320,128]{1,0:T(8,128)S(1)}, f32[320,128]{1,0:T(8,128)S(1)}, u32[]{:S(2)}, u32[]{:S(2)}) collective-permute-start(f32[320,128]{1,0:T(8,128)S(1)} %cores.1.a_ref), channel_id=1, source_target_pairs={{0,2},{2,0},{4,6},{6,4},{8,10},{10,8},{1,3},{3,1},{5,7},{7,5},{9,1... | collective-permute-start | bytes 491528 | tf_op jit(solution)/shard_map/ppermute | solution.py:205
  116.8 4.3 %collective-permute-done.2.b_ref = f32[320,128]{1,0:T(8,128)S(1)} collective-permute-done((f32[320,128]{1,0:T(8,128)S(1)}, f32[320,128]{1,0:T(8,128)S(1)}, u32[]{:S(2)}, u32[]{:S(2)}) %collective-permute-start.2) | collective-permute-done | bytes 163872 | tf_op jit(solution)/shard_map/ppermute | solution.py:205
  121.1 4.1 %collective-permute-start.3 = (bf16[320,128]{1,0:T(8,128)(2,1)S(1)}, bf16[320,128]{1,0:T(8,128)(2,1)S(1)}, u32[]{:S(2)}, u32[]{:S(2)}) collective-permute-start(bf16[320,128]{1,0:T(8,128)(2,1)S(1)} %pairs.1.own_ref), channel_id=1, source_target_pairs={{0,4},{2,6},{4,8},{6,10},{8,0},{10,2},{1,5},{3,7},{5,9},{7,11},{9,... | collective-permute-start | bytes 245768 | tf_op jit(solution)/shard_map/ppermute | solution.py:207
  125.3 8.5 %collective-permute-start.4 = (bf16[320,128]{1,0:T(8,128)(2,1)S(1)}, bf16[320,128]{1,0:T(8,128)(2,1)S(1)}, u32[]{:S(2)}, u32[]{:S(2)}) collective-permute-start(bf16[320,128]{1,0:T(8,128)(2,1)S(1)} %pairs.1.own_ref), channel_id=1, source_target_pairs={{0,8},{2,10},{4,0},{6,2},{8,4},{10,6},{1,9},{3,11},{5,1},{7,3},{9,... | collective-permute-start | bytes 245768 | tf_op jit(solution)/shard_map/ppermute | solution.py:208
  133.8 2.6 %collective-permute-done.3.prev_ref = bf16[320,128]{1,0:T(8,128)(2,1)S(1)} collective-permute-done((bf16[320,128]{1,0:T(8,128)(2,1)S(1)}, bf16[320,128]{1,0:T(8,128)(2,1)S(1)}, u32[]{:S(2)}, u32[]{:S(2)}) %collective-permute-start.3) | collective-permute-done | bytes 81952 | tf_op jit(solution)/shard_map/ppermute | solution.py:207
  136.3 3.6 %collective-permute-done.4.next_ref = bf16[320,128]{1,0:T(8,128)(2,1)S(1)} collective-permute-done((bf16[320,128]{1,0:T(8,128)(2,1)S(1)}, bf16[320,128]{1,0:T(8,128)(2,1)S(1)}, u32[]{:S(2)}, u32[]{:S(2)}) %collective-permute-start.4) | collective-permute-done | bytes 81952 | tf_op jit(solution)/shard_map/ppermute | solution.py:208
  140.0 0.7 triples.1
  140.7 0.0 all-to-all-done.3.got_ref
  140.7 1.3 unpack.1
  (3 shorter events, 0.1 us)
Async XLA Ops:
  53.6 17.1 %collective-permute-start = (bf16[2,40,640]{2,1,0:T(8,128)(2,1)S(1)}, bf16[2,40,640]{2,1,0:T(8,128)(2,1)S(1)}, u32[]{:S(2)}, u32[]{:S(2)}) collective-permute-start(bf16[2,40,640]{2,1,0:T(8,128)(2,1)S(1)} %get-tuple-element.8), channel_id=1, source_target_pairs={{0,12},{12,0},{1,13},{13,1},{2,14},{14,2},{3,15},{15,3},{4,16},{16... | collective-permute-start | bytes 307208 | tf_op jit(solution)/shard_map/ppermute | solution.py:229
  86.7 0.8 copy-start
  87.6 11.7 %all-to-all-start.4 = ((bf16[8,320,128]{2,1,0:T(8,128)(2,1)}), bf16[8,320,128]{2,1,0:T(8,128)(2,1)S(1)}, u32[]{:S(2)}, u32[]{:S(2)}) async-start(bf16[8,320,128]{2,1,0:T(8,128)(2,1)} %copy-done), calls=%async_computation.4 | async-start | bytes 1310720 | tf_op jit(solution)/shard_map/all_to_all | solution.py:198
  99.3 41.4 %all-to-all-start.3 = ((bf16[8,640,128]{2,1,0:T(8,128)(2,1)}), bf16[8,640,128]{2,1,0:T(8,128)(2,1)S(1)}, u32[]{:S(2)}, u32[]{:S(2)}) async-start(bf16[8,640,128]{2,1,0:T(8,128)(2,1)} %grads.1), calls=%async_computation.3 | async-start | bytes 2621440 | tf_op jit(solution)/shard_map/all_to_all | solution.py:198
  102.9 10.2 %collective-permute-start.1 = (f32[320,128]{1,0:T(8,128)S(1)}, f32[320,128]{1,0:T(8,128)S(1)}, u32[]{:S(2)}, u32[]{:S(2)}) collective-permute-start(f32[320,128]{1,0:T(8,128)S(1)} %home.1.a_ref), channel_id=1, source_target_pairs={{0,1},{1,0},{2,3},{3,2},{4,5},{5,4},{6,7},{7,6},{8,9},{9,8},{10,11... | collective-permute-start | bytes 491528 | tf_op jit(solution)/shard_map/ppermute | solution.py:203
  113.1 8.0 %collective-permute-start.2 = (f32[320,128]{1,0:T(8,128)S(1)}, f32[320,128]{1,0:T(8,128)S(1)}, u32[]{:S(2)}, u32[]{:S(2)}) collective-permute-start(f32[320,128]{1,0:T(8,128)S(1)} %cores.1.a_ref), channel_id=1, source_target_pairs={{0,2},{2,0},{4,6},{6,4},{8,10},{10,8},{1,3},{3,1},{5,7},{7,5},{9,1... | collective-permute-start | bytes 491528 | tf_op jit(solution)/shard_map/ppermute | solution.py:205
  121.1 15.2 %collective-permute-start.3 = (bf16[320,128]{1,0:T(8,128)(2,1)S(1)}, bf16[320,128]{1,0:T(8,128)(2,1)S(1)}, u32[]{:S(2)}, u32[]{:S(2)}) collective-permute-start(bf16[320,128]{1,0:T(8,128)(2,1)S(1)} %pairs.1.own_ref), channel_id=1, source_target_pairs={{0,4},{2,6},{4,8},{6,10},{8,0},{10,2},{1,5},{3,7},{5,9},{7,11},{9,... | collective-permute-start | bytes 245768 | tf_op jit(solution)/shard_map/ppermute | solution.py:207
  125.3 14.7 %collective-permute-start.4 = (bf16[320,128]{1,0:T(8,128)(2,1)S(1)}, bf16[320,128]{1,0:T(8,128)(2,1)S(1)}, u32[]{:S(2)}, u32[]{:S(2)}) collective-permute-start(bf16[320,128]{1,0:T(8,128)(2,1)S(1)} %pairs.1.own_ref), channel_id=1, source_target_pairs={{0,8},{2,10},{4,0},{6,2},{8,4},{10,6},{1,9},{3,11},{5,1},{7,3},{9,... | collective-permute-start | bytes 245768 | tf_op jit(solution)/shard_map/ppermute | solution.py:208

commit v3 on v2

--- a/solution.py
+++ b/solution.py
@@ -38,7 +38,7 @@
     )(*args)
 
 
-def pack_kernel(nx, tok_ref, grad_ref, uc_ref, us_ref, dc_ref, ds_ref, out_ref, codes, scales, sems, act_sems):
+def pack_kernel(nx, tok_ref, grad_ref, uc_ref, us_ref, dc_ref, ds_ref, out_ref, codes, scales, packed, sems, act_sems, out_sems):
     feats, units = uc_ref.shape
     width = units // nx
     blocks = width // LANES
@@ -56,17 +56,17 @@
                 side[0].at[:, cols], codes.at[s, :, cols], sems.at[s, x]
             )
             code_copies[s, x].start()
-    act_copies = []
+    pending = []
     for x in range(nx):
         for s, side in enumerate(sides):
-            act_copies.append(
+            pending.append(
                 pltpu.make_async_copy(
                     side[2],
                     out_ref.at[2 * x + s, pl.ds(blocks * feats, tok_ref.shape[0]), :],
                     act_sems.at[2 * x + s],
                 )
             )
-            act_copies[-1].start()
+            pending[-1].start()
     columns = []
     for s in range(2):
         scale_copies[s].wait()
@@ -78,8 +78,16 @@
                 at = (x * blocks + k) * LANES
                 b = at // SCALE_BLOCK
                 w = codes[s, :, at : at + LANES].astype(f32) * columns[s][:, b : b + 1]
-                out_ref[2 * x + s, k * feats : (k + 1) * feats, :] = w.astype(bf16)
-    for copy in act_copies:
+                packed[2 * x + s, k * feats : (k + 1) * feats, :] = w.astype(bf16)
+            pending.append(
+                pltpu.make_async_copy(
+                    packed.at[2 * x + s],
+                    out_ref.at[2 * x + s, pl.ds(0, blocks * feats), :],
+                    out_sems.at[2 * x + s],
+                )
+            )
+            pending[-1].start()
+    for copy in pending:
         copy.wait()
 
 
@@ -91,11 +99,13 @@
         functools.partial(pack_kernel, nx),
         out_shape=jax.ShapeDtypeStruct((2 * nx, rows + tok, LANES), bf16),
         in_specs=[pl.BlockSpec(memory_space=pltpu.HBM)] * 6,
-        out_specs=pl.BlockSpec(memory_space=pltpu.VMEM),
+        out_specs=pl.BlockSpec(memory_space=pltpu.HBM),
         scratch_shapes=[
             pltpu.VMEM((2, feats, units), jnp.int32),
             pltpu.VMEM((2, units // SCALE_BLOCK, feats), f32),
+            pltpu.VMEM((2 * nx, rows, LANES), bf16),
             pltpu.SemaphoreType.DMA((2, nx + 1)),
+            pltpu.SemaphoreType.DMA((2 * nx,)),
             pltpu.SemaphoreType.DMA((2 * nx,)),
         ],
         compiler_params=pltpu.CompilerParams(vmem_limit_bytes=56 * 1024 * 1024),
@@ -138,9 +148,12 @@
         out_ref[2 * h + 1] = hidden
 
 
-def terms_kernel(feats, got_ref, act_ref, out_ref):
+def terms_kernel(feats, theirs, got_ref, act_ref, out_ref):
     blocks = act_ref.shape[1] // LANES
-    act = act_ref[...]
+    half = act_ref.shape[0] // 2
+    core = lax.axis_index("core")
+    start = pl.multiple_of((1 - core if theirs else core) * half, half)
+    act = act_ref[pl.ds(start, half), :]
     for s in range(got_ref.shape[0]):
         total = None
         for k in range(blocks):
@@ -151,7 +164,7 @@
                 preferred_element_type=f32,
             )
             total = part if total is None else total + part
-        out_ref[s] = total.astype(bf16)
+        out_ref[s] = total.astype(out_ref.dtype)
 
 
 def grads_kernel(feats, got_ref, act_ref, out_ref):
@@ -164,15 +177,15 @@
             out_ref[s, k * feats : (k + 1) * feats, :] = grad[:, k * LANES : (k + 1) * LANES].astype(bf16)
 
 
+def pair_kernel(keep_ref, got_ref, out_ref):
+    out_ref[...] = (keep_ref[...] + got_ref[...].astype(f32)).astype(bf16)
+
+
 def home_kernel(got_ref, out_ref):
     total = got_ref[0].astype(f32)
     for x in range(1, got_ref.shape[0] // 2):
         total = total + got_ref[2 * x].astype(f32)
     out_ref[...] = total
-
-
-def pair_kernel(a_ref, b_ref, out_ref):
-    out_ref[...] = (a_ref[...] + b_ref[...]).astype(out_ref.dtype)
 
 
 def triple_kernel(own_ref, prev_ref, next_ref, out_ref):
@@ -184,29 +197,48 @@
     out_ref[...] = (first + second + third).astype(bf16)
 
 
-def unpack_kernel(feats, got_ref, up_ref, down_ref):
+def halves_kernel(own_ref, other_ref, out_ref):
+    half = own_ref.shape[0]
+    core = lax.axis_index("core")
+    out_ref[pl.ds(pl.multiple_of(core * half, half), half), :] = own_ref[...]
+    out_ref[pl.ds(pl.multiple_of((1 - core) * half, half), half), :] = other_ref[...]
+
+
+def unpack_kernel(feats, got_ref, up_ref, down_ref, sems):
     nx = got_ref.shape[0] // 2
     blocks = up_ref.shape[1] // nx // LANES
-    for s, out in enumerate((up_ref, down_ref)):
-        for x in range(nx):
+    copies = []
+    for x in range(nx):
+        for s, out in enumerate((up_ref, down_ref)):
             for k in range(blocks):
-                at = (x * blocks + k) * LANES
-                out[:, at : at + LANES] = got_ref[2 * x + s, k * feats : (k + 1) * feats, :]
+                copies.append(
+                    pltpu.make_async_copy(
+                        got_ref.at[2 * x + s, pl.ds(k * feats, feats), :],
+                        out.at[:, pl.ds((x * blocks + k) * LANES, LANES)],
+                        sems.at[len(copies)],
+                    )
+                )
+                copies[-1].start()
+    for copy in copies:
+        copy.wait()
+
+
+def unpack(feats, units, got):
+    out = jax.ShapeDtypeStruct((feats, units), bf16)
+    hbm = pl.BlockSpec(memory_space=pltpu.HBM)
+    return pl.pallas_call(
+        functools.partial(unpack_kernel, feats),
+        out_shape=(out, out),
+        in_specs=[pl.BlockSpec(memory_space=pltpu.VMEM)],
+        out_specs=(hbm, hbm),
+        scratch_shapes=[pltpu.SemaphoreType.DMA((2 * units // LANES,))],
+        compiler_params=pltpu.CompilerParams(vmem_limit_bytes=48 * 1024 * 1024),
+        name="unpack",
+    )(got)
 
 
 def exchange(value, axes):
     return lax.all_to_all(value, axes, 0, 0, tiled=True)
-
-
-def inter_sum(nzl, ncore, term):
-    S = jax.ShapeDtypeStruct
-    other = lax.ppermute(term, "core", [(i, i ^ 1) for i in range(ncore)])
-    term = call(pair_kernel, S(term.shape, f32), term, other, name="cores")
-    other = lax.ppermute(term, "zl", [(i, i ^ 1) for i in range(nzl)])
-    term = call(pair_kernel, S(term.shape, bf16), term, other, name="pairs")
-    prev = lax.ppermute(term, "zl", [(i, (i + 2) % nzl) for i in range(nzl)])
-    nxt = lax.ppermute(term, "zl", [(i, (i - 2) % nzl) for i in range(nzl)])
-    return call(triple_kernel, S(term.shape, bf16), term, prev, nxt, name="triples")
 
 
 def shards(sizes, tokens, grad_out, up_codes, up_scales, down_codes, down_scales):
@@ -229,17 +261,28 @@
     other = lax.ppermute(send, "zh", [(0, 1), (1, 0)])
     acts = call(gelu_kernel, S((nyh * nyl, share, mine), bf16), keep, other, name="gelu")
     act = exchange(acts, ("yh", "yl")).reshape(tok, mine)
-    terms = call(functools.partial(terms_kernel, feats), S((srcs, tok, feats), bf16), got, act, name="terms")
-    terms = exchange(terms, ("x", "yl"))
+    half = tok // 2
+    swap = [(i, i ^ 1) for i in range(ncore)]
+    send = call(
+        functools.partial(terms_kernel, feats, True), S((srcs, half, feats), bf16), got, act, name="terms_send"
+    )
+    other = lax.ppermute(send, "core", swap)
     grads = call(functools.partial(grads_kernel, feats), S((srcs, rows, LANES), bf16), got, act, name="grads")
+    keep = call(
+        functools.partial(terms_kernel, feats, False), S((srcs, half, feats), f32), got, act, name="terms_keep"
+    )
+    terms = exchange(call(pair_kernel, S((srcs, half, feats), bf16), keep, other, name="pair"), ("x", "yl"))
     home = exchange(grads, ("x", "yl"))
-    grad_tokens = inter_sum(nzl, ncore, call(home_kernel, S((tok, feats), f32), terms, name="home"))
-    grad_up, grad_down = call(
-        functools.partial(unpack_kernel, feats),
-        (S((feats, units), bf16), S((feats, units), bf16)),
-        home,
-        name="unpack",
-    )
+    term = call(home_kernel, S((half, feats), f32), terms, name="home")
+    other = lax.ppermute(term, "zl", [(i, i ^ 1) for i in range(nzl)])
+    term = call(pair_kernel, S((half, feats), bf16), term, other, name="pairs")
+    prev = lax.ppermute(term, "zl", [(i, (i + 2) % nzl) for i in range(nzl)])
+    nxt = lax.ppermute(term, "zl", [(i, (i - 2) % nzl) for i in range(nzl)])
+    final = call(triple_kernel, S((half, feats), bf16), term, prev, nxt, name="triples")
+    grad_tokens = call(
+        halves_kernel, S((tok, feats), bf16), final, lax.ppermute(final, "core", swap), name="halves"
+    )
+    grad_up, grad_down = unpack(feats, units, home)
     return grad_up, grad_down, grad_tokens
 
 

time: 143 us -> 158 us (1.10)
  Pallas kernels: 9.8 us -> 28.3 us
  waiting for transfers between devices: 19.8 us -> 13.4 us
  starting transfers between devices: 47.5 us -> 50.1 us
    pallas_call x1, Pallas kernels: 3.46 us -> 21.2 us  [pack(): pl.pallas_call(functools.partial(pack_kernel, nx), out_shape=jax.ShapeDty...]
    ppermute x4 -> x5, waiting for transfers between devices: 11.5 us -> 5.62 us  [the longest x1 2.44 us: shards(): nxt = lax.ppermute(term, 'zl', [(i, (i - 2) % nzl) for i in range(nzl)])]
    ppermute x4 -> x5, starting transfers between devices: 25.5 us -> 28.3 us  [the longest x1 8 us: shards(): other = lax.ppermute(send, 'core', swap)]
    pallas_call x10 -> x11, Pallas kernels: 6.34 us -> 5.7 us  [call(): pl.pallas_call(kernel, out_shape=out_shape, in_specs=[vmem] * len(args),...]
  transfers between devices with their start and end apart: 7 -> 8, of which waited for: 6 -> 6; matrix products, arithmetic and copies ran while one was open for 0% -> 0% of each run, Pallas kernels for 2% -> 2%
where the time goes in v3:
time: 158 us; the launch traced here: 157 us
  blocking collectives  63.3 us (40%)
  starting transfers between devices  50.1 us (32%)
  Pallas kernels  28.3 us (18%)
  waiting for transfers between devices  13.4 us (8%)
    all_to_all x3, blocking collectives, exchange(): return lax.all_to_all(value, axes, 0, 0, tiled=True)  63.3 us
    pallas_call x1, Pallas kernels, pack(): pl.pallas_call(functools.partial(pack_kernel, nx), out_shape=jax.ShapeDty...  21.2 us
    ppermute x1, starting transfers between devices, shards(): other = lax.ppermute(send, 'zh', [(0, 1), (1, 0)])  14.9 us
    ppermute x1, starting transfers between devices, shards(): other = lax.ppermute(send, 'core', swap)  8 us
    ppermute x1, starting transfers between devices, shards(): nxt = lax.ppermute(term, 'zl', [(i, (i - 2) % nzl) for i in range(nzl)])  7.78 us
    all_to_all x2, starting transfers between devices, exchange(): return lax.all_to_all(value, axes, 0, 0, tiled=True)  7 us
    pallas_call x11, Pallas kernels, call(): pl.pallas_call(kernel, out_shape=out_shape, in_specs=[vmem] * len(args),...  5.7 us
    all_to_all x2, waiting for transfers between devices, exchange(): return lax.all_to_all(value, axes, 0, 0, tiled=True)  5.54 us
  transfers between devices with their start and end apart: 8, of which 6 were waited for; matrix products, arithmetic and copies ran while one was open for 0% of the time, Pallas kernels for 2%

profile of v3, /device:TPU:1, one launch (start us, length us, event | category | flops | bytes accessed | tf_op | source)
XLA Modules:
  0.0 157.0 jit_solution(4916433873517720440)
XLA Ops:
  0.6 21.2 %pack.1 = bf16[8,960,128]{2,1,0:T(8,128)(2,1)} custom-call(bf16[320,128]{1,0:T(8,128)(2,1)} %tok_ref.1, bf16[320,128]{1,0:T(8,128)(2,1)} %grad_ref.1, s32[128,2560]{1,0:T(8,128)} %uc_ref.1, f32[10,128]{1,0:T(8,128)} %bitcast.8, s32[128,2560]{1,0:T(8,128)} %dc_ref.1, f32[10,128]{1,0:T(8,128)} %bitcast.9), custom_call_target="tpu_custom_call" | custom-call | tf_op jit(solution)/shard_map/pack/pallas_call | solution.py:98
  21.9 23.3 %all_to_all.25.got_ref = bf16[8,960,128]{2,1,0:T(8,128)(2,1)S(1)} all-to-all(bf16[8,960,128]{2,1,0:T(8,128)(2,1)} %pack.1), channel_id=1, replica_groups=mesh['x'=4,'yh'=4,'yl'=2,'zh'=2,'zl'=6,'core'=2] {'x','yl'}, dimensions={0} | all-to-all | bytes 3932160 | tf_op jit(solution)/shard_map/all_to_all | solution.py:241
  45.1 1.0 forward.1
  46.1 25.2 %all_to_all.26.got_ref = bf16[8,40,640]{2,1,0:T(8,128)(2,1)S(1)} all-to-all(bf16[8,40,640]{2,1,0:T(8,128)(2,1)S(1)} %bitcast.7), channel_id=1, replica_groups=mesh['x'=4,'yh'=4,'yl'=2,'zh'=2,'zl'=6,'core'=2] {'yh','yl'}, dimensions={0} | all-to-all | bytes 819200 | tf_op jit(solution)/shard_map/all_to_all | solution.py:241
  71.3 0.1 sum.1
  71.3 14.9 %collective-permute-start = (bf16[2,40,640]{2,1,0:T(8,128)(2,1)S(1)}, bf16[2,40,640]{2,1,0:T(8,128)(2,1)S(1)}, u32[]{:S(2)}, u32[]{:S(2)}) collective-permute-start(bf16[2,40,640]{2,1,0:T(8,128)(2,1)S(1)} %get-tuple-element.8), channel_id=1, source_target_pairs={{0,12},{12,0},{1,13},{13,1},{2,14},{14,2},{3,15},{15,3},{4,16},{16... | collective-permute-start | bytes 307208 | tf_op jit(solution)/shard_map/ppermute | solution.py:261
  86.2 2.2 %collective-permute-done.got_ref = bf16[2,40,640]{2,1,0:T(8,128)(2,1)S(1)} collective-permute-done((bf16[2,40,640]{2,1,0:T(8,128)(2,1)S(1)}, bf16[2,40,640]{2,1,0:T(8,128)(2,1)S(1)}, u32[]{:S(2)}, u32[]{:S(2)}) %collective-permute-start) | collective-permute-done | bytes 102432 | tf_op jit(solution)/shard_map/ppermute | solution.py:261
  88.4 0.1 gelu.1
  88.6 14.9 %all_to_all.27 = bf16[8,40,640]{2,1,0:T(8,128)(2,1)S(1)} all-to-all(bf16[8,40,640]{2,1,0:T(8,128)(2,1)S(1)} %gelu.1), channel_id=1, replica_groups=mesh['x'=4,'yh'=4,'yl'=2,'zh'=2,'zl'=6,'core'=2] {'yh','yl'}, dimensions={0} | all-to-all | bytes 819200 | tf_op jit(solution)/shard_map/all_to_all | solution.py:241
  103.4 1.0 terms_send.1
  104.5 8.0 %collective-permute-start.1 = (bf16[8,160,128]{2,1,0:T(8,128)(2,1)S(1)}, bf16[8,160,128]{2,1,0:T(8,128)(2,1)S(1)}, u32[]{:S(2)}, u32[]{:S(2)}) collective-permute-start(bf16[8,160,128]{2,1,0:T(8,128)(2,1)S(1)} %terms_send.1), channel_id=1, source_target_pairs={{0,1},{1,0},{2,3},{3,2},{4,5},{5,4},{6,7},{7,6},{8,9},{9,8},{10,11... | collective-permute-start | bytes 983048 | tf_op jit(solution)/shard_map/ppermute | solution.py:269
  112.5 1.0 terms_keep.1.keep_ref
  113.5 0.2 collective-permute-done.1.got_ref
  113.7 0.8 pair.1
  114.5 3.4 %all-to-all-start.4 = ((bf16[8,160,128]{2,1,0:T(8,128)(2,1)}), bf16[8,160,128]{2,1,0:T(8,128)(2,1)S(1)}, u32[]{:S(2)}, u32[]{:S(2)}) async-start(bf16[8,160,128]{2,1,0:T(8,128)(2,1)} %pair.1), calls=%async_computation.4 | async-start | bytes 655360 | tf_op jit(solution)/shard_map/all_to_all | solution.py:241
  117.9 1.0 grads.1
  119.0 0.0 copy-start
  119.0 1.1 copy-done
  120.0 5.5 %all-to-all-done.4.got_ref = bf16[8,160,128]{2,1,0:T(8,128)(2,1)S(1)} async-done(((bf16[8,160,128]{2,1,0:T(8,128)(2,1)}), bf16[8,160,128]{2,1,0:T(8,128)(2,1)S(1)}, u32[]{:S(2)}, u32[]{:S(2)}) %all-to-all-start.4) | async-done | bytes 327712 | tf_op jit(solution)/shard_map/all_to_all | solution.py:241
  125.6 3.6 %all-to-all-start.3 = ((bf16[8,640,128]{2,1,0:T(8,128)(2,1)}), bf16[8,640,128]{2,1,0:T(8,128)(2,1)S(1)}, u32[]{:S(2)}, u32[]{:S(2)}) async-start(bf16[8,640,128]{2,1,0:T(8,128)(2,1)} %copy-done), calls=%async_computation.3 | async-start | bytes 2621440 | tf_op jit(solution)/shard_map/all_to_all | solution.py:241
  129.2 3.7 %collective-permute-start.2 = (f32[160,128]{1,0:T(8,128)S(1)}, f32[160,128]{1,0:T(8,128)S(1)}, u32[]{:S(2)}, u32[]{:S(2)}) collective-permute-start(f32[160,128]{1,0:T(8,128)S(1)} %home.1.keep_ref), channel_id=1, source_target_pairs={{0,2},{2,0},{4,6},{6,4},{8,10},{10,8},{1,3},{3,1},{5,7},{7,5},{9,1... | collective-permute-start | bytes 245768 | tf_op jit(solution)/shard_map/ppermute | solution.py:277
  132.9 2.1 %collective-permute-done.2.got_ref = f32[160,128]{1,0:T(8,128)S(1)} collective-permute-done((f32[160,128]{1,0:T(8,128)S(1)}, f32[160,128]{1,0:T(8,128)S(1)}, u32[]{:S(2)}, u32[]{:S(2)}) %collective-permute-start.2) | collective-permute-done | bytes 81952 | tf_op jit(solution)/shard_map/ppermute | solution.py:277
  135.1 4.5 %collective-permute-start.3 = (bf16[160,128]{1,0:T(8,128)(2,1)S(1)}, bf16[160,128]{1,0:T(8,128)(2,1)S(1)}, u32[]{:S(2)}, u32[]{:S(2)}) collective-permute-start(bf16[160,128]{1,0:T(8,128)(2,1)S(1)} %pairs.1.own_ref), channel_id=1, source_target_pairs={{0,4},{2,6},{4,8},{6,10},{8,0},{10,2},{1,5},{3,7},{5,9},{7,11},{9,... | collective-permute-start | bytes 122888 | tf_op jit(solution)/shard_map/ppermute | solution.py:279
  139.5 7.8 %collective-permute-start.4 = (bf16[160,128]{1,0:T(8,128)(2,1)S(1)}, bf16[160,128]{1,0:T(8,128)(2,1)S(1)}, u32[]{:S(2)}, u32[]{:S(2)}) collective-permute-start(bf16[160,128]{1,0:T(8,128)(2,1)S(1)} %pairs.1.own_ref), channel_id=1, source_target_pairs={{0,8},{2,10},{4,0},{6,2},{8,4},{10,6},{1,9},{3,11},{5,1},{7,3},{9,... | collective-permute-start | bytes 122888 | tf_op jit(solution)/shard_map/ppermute | solution.py:280
  147.3 0.0 collective-permute-done.3.prev_ref
  147.3 2.4 %collective-permute-done.4.next_ref = bf16[160,128]{1,0:T(8,128)(2,1)S(1)} collective-permute-done((bf16[160,128]{1,0:T(8,128)(2,1)S(1)}, bf16[160,128]{1,0:T(8,128)(2,1)S(1)}, u32[]{:S(2)}, u32[]{:S(2)}) %collective-permute-start.4) | collective-permute-done | bytes 40992 | tf_op jit(solution)/shard_map/ppermute | solution.py:280
  149.8 4.3 %collective-permute-start.5 = (bf16[160,128]{1,0:T(8,128)(2,1)S(1)}, bf16[160,128]{1,0:T(8,128)(2,1)S(1)}, u32[]{:S(2)}, u32[]{:S(2)}) collective-permute-start(bf16[160,128]{1,0:T(8,128)(2,1)S(1)} %triples.1.own_ref), channel_id=1, source_target_pairs={{0,1},{1,0},{2,3},{3,2},{4,5},{5,4},{6,7},{7,6},{8,9},{9,8},{10,11... | collective-permute-start | bytes 122888 | tf_op jit(solution)/shard_map/ppermute | solution.py:283
  154.1 0.8 collective-permute-done.5.other_ref
  155.0 0.6 halves.1
  155.6 0.0 all-to-all-done.3.got_ref
  155.6 1.4 unpack.1
  (3 shorter events, 0.1 us)
Async XLA Ops:
  71.3 17.1 %collective-permute-start = (bf16[2,40,640]{2,1,0:T(8,128)(2,1)S(1)}, bf16[2,40,640]{2,1,0:T(8,128)(2,1)S(1)}, u32[]{:S(2)}, u32[]{:S(2)}) collective-permute-start(bf16[2,40,640]{2,1,0:T(8,128)(2,1)S(1)} %get-tuple-element.8), channel_id=1, source_target_pairs={{0,12},{12,0},{1,13},{13,1},{2,14},{14,2},{3,15},{15,3},{4,16},{16... | collective-permute-start | bytes 307208 | tf_op jit(solution)/shard_map/ppermute | solution.py:261
  104.5 9.2 %collective-permute-start.1 = (bf16[8,160,128]{2,1,0:T(8,128)(2,1)S(1)}, bf16[8,160,128]{2,1,0:T(8,128)(2,1)S(1)}, u32[]{:S(2)}, u32[]{:S(2)}) collective-permute-start(bf16[8,160,128]{2,1,0:T(8,128)(2,1)S(1)} %terms_send.1), channel_id=1, source_target_pairs={{0,1},{1,0},{2,3},{3,2},{4,5},{5,4},{6,7},{7,6},{8,9},{9,8},{10,11... | collective-permute-start | bytes 983048 | tf_op jit(solution)/shard_map/ppermute | solution.py:269
  114.5 11.1 %all-to-all-start.4 = ((bf16[8,160,128]{2,1,0:T(8,128)(2,1)}), bf16[8,160,128]{2,1,0:T(8,128)(2,1)S(1)}, u32[]{:S(2)}, u32[]{:S(2)}) async-start(bf16[8,160,128]{2,1,0:T(8,128)(2,1)} %pair.1), calls=%async_computation.4 | async-start | bytes 655360 | tf_op jit(solution)/shard_map/all_to_all | solution.py:241
  119.0 1.1 copy-start
  125.6 30.0 %all-to-all-start.3 = ((bf16[8,640,128]{2,1,0:T(8,128)(2,1)}), bf16[8,640,128]{2,1,0:T(8,128)(2,1)S(1)}, u32[]{:S(2)}, u32[]{:S(2)}) async-start(bf16[8,640,128]{2,1,0:T(8,128)(2,1)} %copy-done), calls=%async_computation.3 | async-start | bytes 2621440 | tf_op jit(solution)/shard_map/all_to_all | solution.py:241
  129.2 5.9 %collective-permute-start.2 = (f32[160,128]{1,0:T(8,128)S(1)}, f32[160,128]{1,0:T(8,128)S(1)}, u32[]{:S(2)}, u32[]{:S(2)}) collective-permute-start(f32[160,128]{1,0:T(8,128)S(1)} %home.1.keep_ref), channel_id=1, source_target_pairs={{0,2},{2,0},{4,6},{6,4},{8,10},{10,8},{1,3},{3,1},{5,7},{7,5},{9,1... | collective-permute-start | bytes 245768 | tf_op jit(solution)/shard_map/ppermute | solution.py:277
  135.1 12.2 %collective-permute-start.3 = (bf16[160,128]{1,0:T(8,128)(2,1)S(1)}, bf16[160,128]{1,0:T(8,128)(2,1)S(1)}, u32[]{:S(2)}, u32[]{:S(2)}) collective-permute-start(bf16[160,128]{1,0:T(8,128)(2,1)S(1)} %pairs.1.own_ref), channel_id=1, source_target_pairs={{0,4},{2,6},{4,8},{6,10},{8,0},{10,2},{1,5},{3,7},{5,9},{7,11},{9,... | collective-permute-start | bytes 122888 | tf_op jit(solution)/shard_map/ppermute | solution.py:279
  139.5 10.2 %collective-permute-start.4 = (bf16[160,128]{1,0:T(8,128)(2,1)S(1)}, bf16[160,128]{1,0:T(8,128)(2,1)S(1)}, u32[]{:S(2)}, u32[]{:S(2)}) collective-permute-start(bf16[160,128]{1,0:T(8,128)(2,1)S(1)} %pairs.1.own_ref), channel_id=1, source_target_pairs={{0,8},{2,10},{4,0},{6,2},{8,4},{10,6},{1,9},{3,11},{5,1},{7,3},{9,... | collective-permute-start | bytes 122888 | tf_op jit(solution)/shard_map/ppermute | solution.py:280
  149.8 5.2 %collective-permute-start.5 = (bf16[160,128]{1,0:T(8,128)(2,1)S(1)}, bf16[160,128]{1,0:T(8,128)(2,1)S(1)}, u32[]{:S(2)}, u32[]{:S(2)}) collective-permute-start(bf16[160,128]{1,0:T(8,128)(2,1)S(1)} %triples.1.own_ref), channel_id=1, source_target_pairs={{0,1},{1,0},{2,3},{3,2},{4,5},{5,4},{6,7},{7,6},{8,9},{9,8},{10,11... | collective-permute-start | bytes 122888 | tf_op jit(solution)/shard_map/ppermute | solution.py:283

commit v4 on v3

--- a/solution.py
+++ b/solution.py
@@ -38,7 +38,7 @@
     )(*args)
 
 
-def pack_kernel(nx, tok_ref, grad_ref, uc_ref, us_ref, dc_ref, ds_ref, out_ref, codes, scales, packed, sems, act_sems, out_sems):
+def pack_kernel(nx, tok_ref, grad_ref, uc_ref, us_ref, dc_ref, ds_ref, out_ref, codes, scales, acts, packed, sems, act_sems, out_sems):
     feats, units = uc_ref.shape
     width = units // nx
     blocks = width // LANES
@@ -56,21 +56,18 @@
                 side[0].at[:, cols], codes.at[s, :, cols], sems.at[s, x]
             )
             code_copies[s, x].start()
+    act_copies = [pltpu.make_async_copy(side[2], acts.at[s], act_sems.at[s]) for s, side in enumerate(sides)]
+    for copy in act_copies:
+        copy.start()
     pending = []
-    for x in range(nx):
-        for s, side in enumerate(sides):
-            pending.append(
-                pltpu.make_async_copy(
-                    side[2],
-                    out_ref.at[2 * x + s, pl.ds(blocks * feats, tok_ref.shape[0]), :],
-                    act_sems.at[2 * x + s],
-                )
-            )
-            pending[-1].start()
     columns = []
     for s in range(2):
         scale_copies[s].wait()
         columns.append(scales[s].T)
+    for s in range(2):
+        act_copies[s].wait()
+        for x in range(nx):
+            packed[2 * x + s, blocks * feats :, :] = acts[s]
     for x in range(nx):
         for s in range(2):
             code_copies[s, x].wait()
@@ -81,9 +78,7 @@
                 packed[2 * x + s, k * feats : (k + 1) * feats, :] = w.astype(bf16)
             pending.append(
                 pltpu.make_async_copy(
-                    packed.at[2 * x + s],
-                    out_ref.at[2 * x + s, pl.ds(0, blocks * feats), :],
-                    out_sems.at[2 * x + s],
+                    packed.at[2 * x + s], out_ref.at[2 * x + s], out_sems.at[2 * x + s]
                 )
             )
             pending[-1].start()
@@ -103,9 +98,10 @@
         scratch_shapes=[
             pltpu.VMEM((2, feats, units), jnp.int32),
             pltpu.VMEM((2, units // SCALE_BLOCK, feats), f32),
-            pltpu.VMEM((2 * nx, rows, LANES), bf16),
+            pltpu.VMEM((2, tok, LANES), bf16),
+            pltpu.VMEM((2 * nx, rows + tok, LANES), bf16),
             pltpu.SemaphoreType.DMA((2, nx + 1)),
-            pltpu.SemaphoreType.DMA((2 * nx,)),
+            pltpu.SemaphoreType.DMA((2,)),
             pltpu.SemaphoreType.DMA((2 * nx,)),
         ],
         compiler_params=pltpu.CompilerParams(vmem_limit_bytes=56 * 1024 * 1024),
@@ -272,10 +268,11 @@
         functools.partial(terms_kernel, feats, False), S((srcs, half, feats), f32), got, act, name="terms_keep"
     )
     terms = exchange(call(pair_kernel, S((srcs, half, feats), bf16), keep, other, name="pair"), ("x", "yl"))
-    home = exchange(grads, ("x", "yl"))
     term = call(home_kernel, S((half, feats), f32), terms, name="home")
     other = lax.ppermute(term, "zl", [(i, i ^ 1) for i in range(nzl)])
     term = call(pair_kernel, S((half, feats), bf16), term, other, name="pairs")
+    term, grads = lax.optimization_barrier((term, grads))
+    home = exchange(grads, ("x", "yl"))
     prev = lax.ppermute(term, "zl", [(i, (i + 2) % nzl) for i in range(nzl)])
     nxt = lax.ppermute(term, "zl", [(i, (i - 2) % nzl) for i in range(nzl)])
     final = call(triple_kernel, S((half, feats), bf16), term, prev, nxt, name="triples")

time: 158 us -> 138 us (0.87)
  Pallas kernels: 28.3 us -> 11 us
  blocking collectives: 63.3 us -> 73.2 us
  waiting for transfers between devices: 13.4 us -> 6.56 us
  starting transfers between devices: 50.1 us -> 46.2 us
    pallas_call x1, Pallas kernels: 21.2 us -> 3.57 us  [pack(): pl.pallas_call(functools.partial(pack_kernel, nx), out_shape=jax.ShapeDty...]
    all_to_all x3 -> x4, blocking collectives: 63.3 us -> 73.2 us  [exchange(): return lax.all_to_all(value, axes, 0, 0, tiled=True)]
    all_to_all x2 -> x1, waiting for transfers between devices: 5.54 us -> 0.01 us  [exchange(): return lax.all_to_all(value, axes, 0, 0, tiled=True)]
    all_to_all x2 -> x1, starting transfers between devices: 7 us -> 3.58 us  [exchange(): return lax.all_to_all(value, axes, 0, 0, tiled=True)]
    ppermute x1, waiting for transfers between devices: 2.11 us -> 0.01 us  [shards(): other = lax.ppermute(term, 'zl', [(i, i ^ 1) for i in range(nzl)])]
  transfers between devices with their start and end apart: 8 -> 7, of which waited for: 6 -> 4; matrix products, arithmetic and copies ran while one was open for 0% -> 0% of each run, Pallas kernels for 2% -> 3%
where the time goes in v4:
time: 138 us
  blocking collectives  73.2 us (53%)
  starting transfers between devices  46.2 us (33%)
  Pallas kernels  11 us (8%)
  waiting for transfers between devices  6.56 us (5%)
    all_to_all x4, blocking collectives, exchange(): return lax.all_to_all(value, axes, 0, 0, tiled=True)  73.2 us
    ppermute x1, starting transfers between devices, shards(): other = lax.ppermute(send, 'zh', [(0, 1), (1, 0)])  14.9 us
    ppermute x1, starting transfers between devices, shards(): other = lax.ppermute(send, 'core', swap)  7.99 us
    ppermute x1, starting transfers between devices, shards(): nxt = lax.ppermute(term, 'zl', [(i, (i - 2) % nzl) for i in range(nzl)])  7.78 us
    pallas_call x11, Pallas kernels, call(): pl.pallas_call(kernel, out_shape=out_shape, in_specs=[vmem] * len(args),...  6.05 us
    ppermute x1, starting transfers between devices, shards(): prev = lax.ppermute(term, 'zl', [(i, (i + 2) % nzl) for i in range(nzl)])  4.16 us
    ppermute x1, starting transfers between devices, shards(): lax.ppermute(final, 'core', swap)  4.12 us
    ppermute x1, starting transfers between devices, shards(): other = lax.ppermute(term, 'zl', [(i, i ^ 1) for i in range(nzl)])  3.73 us
  transfers between devices with their start and end apart: 7, of which 4 were waited for; matrix products, arithmetic and copies ran while one was open for 0% of the time, Pallas kernels for 3%

profile of v4, /device:TPU:1, one launch (start us, length us, event | category | flops | bytes accessed | tf_op | source)
XLA Modules:
  0.0 137.8 jit_solution(1103911497945203615)
XLA Ops:
  0.6 3.6 %pack.1 = bf16[8,960,128]{2,1,0:T(8,128)(2,1)} custom-call(bf16[320,128]{1,0:T(8,128)(2,1)} %tok_ref.1, bf16[320,128]{1,0:T(8,128)(2,1)} %grad_ref.1, s32[128,2560]{1,0:T(8,128)} %uc_ref.1, f32[10,128]{1,0:T(8,128)} %bitcast.8, s32[128,2560]{1,0:T(8,128)} %dc_ref.1, f32[10,128]{1,0:T(8,128)} %bitcast.9), custom_call_target="tpu_custom_call" | custom-call | tf_op jit(solution)/shard_map/pack/pallas_call | solution.py:93
  4.2 23.3 %all_to_all.25.got_ref = bf16[8,960,128]{2,1,0:T(8,128)(2,1)S(1)} all-to-all(bf16[8,960,128]{2,1,0:T(8,128)(2,1)} %pack.1), channel_id=1, replica_groups=mesh['x'=4,'yh'=4,'yl'=2,'zh'=2,'zl'=6,'core'=2] {'x','yl'}, dimensions={0} | all-to-all | bytes 3932160 | tf_op jit(solution)/shard_map/all_to_all | solution.py:237
  27.5 1.0 forward.1
  28.5 25.2 %all_to_all.26.got_ref = bf16[8,40,640]{2,1,0:T(8,128)(2,1)S(1)} all-to-all(bf16[8,40,640]{2,1,0:T(8,128)(2,1)S(1)} %bitcast.7), channel_id=1, replica_groups=mesh['x'=4,'yh'=4,'yl'=2,'zh'=2,'zl'=6,'core'=2] {'yh','yl'}, dimensions={0} | all-to-all | bytes 819200 | tf_op jit(solution)/shard_map/all_to_all | solution.py:237
  53.6 0.1 sum.1
  53.7 14.9 %collective-permute-start = (bf16[2,40,640]{2,1,0:T(8,128)(2,1)S(1)}, bf16[2,40,640]{2,1,0:T(8,128)(2,1)S(1)}, u32[]{:S(2)}, u32[]{:S(2)}) collective-permute-start(bf16[2,40,640]{2,1,0:T(8,128)(2,1)S(1)} %get-tuple-element.10), channel_id=1, source_target_pairs={{0,12},{12,0},{1,13},{13,1},{2,14},{14,2},{3,15},{15,3},{4,16},{16... | collective-permute-start | bytes 307208 | tf_op jit(solution)/shard_map/ppermute | solution.py:257
  68.6 2.2 %collective-permute-done.got_ref = bf16[2,40,640]{2,1,0:T(8,128)(2,1)S(1)} collective-permute-done((bf16[2,40,640]{2,1,0:T(8,128)(2,1)S(1)}, bf16[2,40,640]{2,1,0:T(8,128)(2,1)S(1)}, u32[]{:S(2)}, u32[]{:S(2)}) %collective-permute-start) | collective-permute-done | bytes 102432 | tf_op jit(solution)/shard_map/ppermute | solution.py:257
  70.8 0.1 gelu.1
  70.9 14.9 %all_to_all.27 = bf16[8,40,640]{2,1,0:T(8,128)(2,1)S(1)} all-to-all(bf16[8,40,640]{2,1,0:T(8,128)(2,1)S(1)} %gelu.1), channel_id=1, replica_groups=mesh['x'=4,'yh'=4,'yl'=2,'zh'=2,'zl'=6,'core'=2] {'yh','yl'}, dimensions={0} | all-to-all | bytes 819200 | tf_op jit(solution)/shard_map/all_to_all | solution.py:237
  85.8 1.0 terms_send.1
  86.8 8.0 %collective-permute-start.1 = (bf16[8,160,128]{2,1,0:T(8,128)(2,1)S(1)}, bf16[8,160,128]{2,1,0:T(8,128)(2,1)S(1)}, u32[]{:S(2)}, u32[]{:S(2)}) collective-permute-start(bf16[8,160,128]{2,1,0:T(8,128)(2,1)S(1)} %terms_send.1), channel_id=1, source_target_pairs={{0,1},{1,0},{2,3},{3,2},{4,5},{5,4},{6,7},{7,6},{8,9},{9,8},{10,11... | collective-permute-start | bytes 983048 | tf_op jit(solution)/shard_map/ppermute | solution.py:265
  94.8 1.0 terms_keep.1.keep_ref
  95.8 0.2 collective-permute-done.1.got_ref
  96.1 0.1 pair.1
  96.1 9.9 %all_to_all.28.got_ref = bf16[8,160,128]{2,1,0:T(8,128)(2,1)S(1)} all-to-all(bf16[8,160,128]{2,1,0:T(8,128)(2,1)S(1)} %pair.1), channel_id=1, replica_groups=mesh['x'=4,'yh'=4,'yl'=2,'zh'=2,'zl'=6,'core'=2] {'x','yl'}, dimensions={0} | all-to-all | bytes 655360 | tf_op jit(solution)/shard_map/all_to_all | solution.py:237
  106.0 3.7 %collective-permute-start.2 = (f32[160,128]{1,0:T(8,128)S(1)}, f32[160,128]{1,0:T(8,128)S(1)}, u32[]{:S(2)}, u32[]{:S(2)}) collective-permute-start(f32[160,128]{1,0:T(8,128)S(1)} %home.1.keep_ref), channel_id=1, source_target_pairs={{0,2},{2,0},{4,6},{6,4},{8,10},{10,8},{1,3},{3,1},{5,7},{7,5},{9,1... | collective-permute-start | bytes 245768 | tf_op jit(solution)/shard_map/ppermute | solution.py:272
  109.8 2.1 %grads.1 = bf16[8,640,128]{2,1,0:T(8,128)(2,1)} custom-call(bf16[8,960,128]{2,1,0:T(8,128)(2,1)S(1)} %all_to_all.25.got_ref, bf16[320,640]{1,0:T(8,128)(2,1)S(1)} %bitcast.6), custom_call_target="tpu_custom_call" | custom-call | tf_op jit(solution)/shard_map/grads/pallas_call | solution.py:31
  111.9 0.0 collective-permute-done.2.got_ref
  111.9 3.6 %all-to-all-start.4 = ((bf16[8,640,128]{2,1,0:T(8,128)(2,1)}), bf16[8,640,128]{2,1,0:T(8,128)(2,1)S(1)}, u32[]{:S(2)}, u32[]{:S(2)}) async-start(bf16[8,640,128]{2,1,0:T(8,128)(2,1)} %grads.1), calls=%async_computation.4 | async-start | bytes 2621440 | tf_op jit(solution)/shard_map/all_to_all | solution.py:237
  115.5 4.2 %collective-permute-start.3 = (bf16[160,128]{1,0:T(8,128)(2,1)S(1)}, bf16[160,128]{1,0:T(8,128)(2,1)S(1)}, u32[]{:S(2)}, u32[]{:S(2)}) collective-permute-start(bf16[160,128]{1,0:T(8,128)(2,1)S(1)} %pairs.1.own_ref), channel_id=1, source_target_pairs={{0,4},{2,6},{4,8},{6,10},{8,0},{10,2},{1,5},{3,7},{5,9},{7,11},{9,... | collective-permute-start | bytes 122888 | tf_op jit(solution)/shard_map/ppermute | solution.py:276
  119.7 7.8 %collective-permute-start.4 = (bf16[160,128]{1,0:T(8,128)(2,1)S(1)}, bf16[160,128]{1,0:T(8,128)(2,1)S(1)}, u32[]{:S(2)}, u32[]{:S(2)}) collective-permute-start(bf16[160,128]{1,0:T(8,128)(2,1)S(1)} %pairs.1.own_ref), channel_id=1, source_target_pairs={{0,8},{2,10},{4,0},{6,2},{8,4},{10,6},{1,9},{3,11},{5,1},{7,3},{9,... | collective-permute-start | bytes 122888 | tf_op jit(solution)/shard_map/ppermute | solution.py:277
  127.5 0.0 collective-permute-done.3.prev_ref
  127.5 3.2 %collective-permute-done.4.next_ref = bf16[160,128]{1,0:T(8,128)(2,1)S(1)} collective-permute-done((bf16[160,128]{1,0:T(8,128)(2,1)S(1)}, bf16[160,128]{1,0:T(8,128)(2,1)S(1)}, u32[]{:S(2)}, u32[]{:S(2)}) %collective-permute-start.4) | collective-permute-done | bytes 40992 | tf_op jit(solution)/shard_map/ppermute | solution.py:277
  130.8 4.1 %collective-permute-start.5 = (bf16[160,128]{1,0:T(8,128)(2,1)S(1)}, bf16[160,128]{1,0:T(8,128)(2,1)S(1)}, u32[]{:S(2)}, u32[]{:S(2)}) collective-permute-start(bf16[160,128]{1,0:T(8,128)(2,1)S(1)} %triples.1.own_ref), channel_id=1, source_target_pairs={{0,1},{1,0},{2,3},{3,2},{4,5},{5,4},{6,7},{7,6},{8,9},{9,8},{10,11... | collective-permute-start | bytes 122888 | tf_op jit(solution)/shard_map/ppermute | solution.py:280
  134.9 0.8 collective-permute-done.5.other_ref
  135.7 0.6 halves.1
  136.4 0.0 all-to-all-done.4.got_ref
  136.4 1.4 %unpack.1 = (bf16[128,2560]{1,0:T(8,128)(2,1)}, bf16[128,2560]{1,0:T(8,128)(2,1)}) custom-call(bf16[8,640,128]{2,1,0:T(8,128)(2,1)S(1)} %all-to-all-done.4.got_ref), custom_call_target="tpu_custom_call" | custom-call | tf_op jit(solution)/shard_map/unpack/pallas_call | solution.py:225
  (3 shorter events, 0.1 us)
Async XLA Ops:
  53.7 17.1 %collective-permute-start = (bf16[2,40,640]{2,1,0:T(8,128)(2,1)S(1)}, bf16[2,40,640]{2,1,0:T(8,128)(2,1)S(1)}, u32[]{:S(2)}, u32[]{:S(2)}) collective-permute-start(bf16[2,40,640]{2,1,0:T(8,128)(2,1)S(1)} %get-tuple-element.10), channel_id=1, source_target_pairs={{0,12},{12,0},{1,13},{13,1},{2,14},{14,2},{3,15},{15,3},{4,16},{16... | collective-permute-start | bytes 307208 | tf_op jit(solution)/shard_map/ppermute | solution.py:257
  86.8 9.2 %collective-permute-start.1 = (bf16[8,160,128]{2,1,0:T(8,128)(2,1)S(1)}, bf16[8,160,128]{2,1,0:T(8,128)(2,1)S(1)}, u32[]{:S(2)}, u32[]{:S(2)}) collective-permute-start(bf16[8,160,128]{2,1,0:T(8,128)(2,1)S(1)} %terms_send.1), channel_id=1, source_target_pairs={{0,1},{1,0},{2,3},{3,2},{4,5},{5,4},{6,7},{7,6},{8,9},{9,8},{10,11... | collective-permute-start | bytes 983048 | tf_op jit(solution)/shard_map/ppermute | solution.py:265
  106.0 5.9 %collective-permute-start.2 = (f32[160,128]{1,0:T(8,128)S(1)}, f32[160,128]{1,0:T(8,128)S(1)}, u32[]{:S(2)}, u32[]{:S(2)}) collective-permute-start(f32[160,128]{1,0:T(8,128)S(1)} %home.1.keep_ref), channel_id=1, source_target_pairs={{0,2},{2,0},{4,6},{6,4},{8,10},{10,8},{1,3},{3,1},{5,7},{7,5},{9,1... | collective-permute-start | bytes 245768 | tf_op jit(solution)/shard_map/ppermute | solution.py:272
  111.9 24.5 %all-to-all-start.4 = ((bf16[8,640,128]{2,1,0:T(8,128)(2,1)}), bf16[8,640,128]{2,1,0:T(8,128)(2,1)S(1)}, u32[]{:S(2)}, u32[]{:S(2)}) async-start(bf16[8,640,128]{2,1,0:T(8,128)(2,1)} %grads.1), calls=%async_computation.4 | async-start | bytes 2621440 | tf_op jit(solution)/shard_map/all_to_all | solution.py:237
  115.5 12.0 %collective-permute-start.3 = (bf16[160,128]{1,0:T(8,128)(2,1)S(1)}, bf16[160,128]{1,0:T(8,128)(2,1)S(1)}, u32[]{:S(2)}, u32[]{:S(2)}) collective-permute-start(bf16[160,128]{1,0:T(8,128)(2,1)S(1)} %pairs.1.own_ref), channel_id=1, source_target_pairs={{0,4},{2,6},{4,8},{6,10},{8,0},{10,2},{1,5},{3,7},{5,9},{7,11},{9,... | collective-permute-start | bytes 122888 | tf_op jit(solution)/shard_map/ppermute | solution.py:276
  119.7 11.0 %collective-permute-start.4 = (bf16[160,128]{1,0:T(8,128)(2,1)S(1)}, bf16[160,128]{1,0:T(8,128)(2,1)S(1)}, u32[]{:S(2)}, u32[]{:S(2)}) collective-permute-start(bf16[160,128]{1,0:T(8,128)(2,1)S(1)} %pairs.1.own_ref), channel_id=1, source_target_pairs={{0,8},{2,10},{4,0},{6,2},{8,4},{10,6},{1,9},{3,11},{5,1},{7,3},{9,... | collective-permute-start | bytes 122888 | tf_op jit(solution)/shard_map/ppermute | solution.py:277
  130.8 5.0 %collective-permute-start.5 = (bf16[160,128]{1,0:T(8,128)(2,1)S(1)}, bf16[160,128]{1,0:T(8,128)(2,1)S(1)}, u32[]{:S(2)}, u32[]{:S(2)}) collective-permute-start(bf16[160,128]{1,0:T(8,128)(2,1)S(1)} %triples.1.own_ref), channel_id=1, source_target_pairs={{0,1},{1,0},{2,3},{3,2},{4,5},{5,4},{6,7},{7,6},{8,9},{9,8},{10,11... | collective-permute-start | bytes 122888 | tf_op jit(solution)/shard_map/ppermute | solution.py:280

commit v5 on v4

--- a/solution.py
+++ b/solution.py
@@ -64,10 +64,6 @@
     for s in range(2):
         scale_copies[s].wait()
         columns.append(scales[s].T)
-    for s in range(2):
-        act_copies[s].wait()
-        for x in range(nx):
-            packed[2 * x + s, blocks * feats :, :] = acts[s]
     for x in range(nx):
         for s in range(2):
             code_copies[s, x].wait()
@@ -78,7 +74,20 @@
                 packed[2 * x + s, k * feats : (k + 1) * feats, :] = w.astype(bf16)
             pending.append(
                 pltpu.make_async_copy(
-                    packed.at[2 * x + s], out_ref.at[2 * x + s], out_sems.at[2 * x + s]
+                    packed.at[2 * x + s],
+                    out_ref.at[2 * x + s, pl.ds(0, blocks * feats), :],
+                    out_sems.at[0, 2 * x + s],
+                )
+            )
+            pending[-1].start()
+    for s in range(2):
+        act_copies[s].wait()
+        for x in range(nx):
+            pending.append(
+                pltpu.make_async_copy(
+                    acts.at[s],
+                    out_ref.at[2 * x + s, pl.ds(blocks * feats, tok_ref.shape[0]), :],
+                    out_sems.at[1, 2 * x + s],
                 )
             )
             pending[-1].start()
@@ -99,29 +108,37 @@
             pltpu.VMEM((2, feats, units), jnp.int32),
             pltpu.VMEM((2, units // SCALE_BLOCK, feats), f32),
             pltpu.VMEM((2, tok, LANES), bf16),
-            pltpu.VMEM((2 * nx, rows + tok, LANES), bf16),
+            pltpu.VMEM((2 * nx, rows, LANES), bf16),
             pltpu.SemaphoreType.DMA((2, nx + 1)),
             pltpu.SemaphoreType.DMA((2,)),
-            pltpu.SemaphoreType.DMA((2 * nx,)),
+            pltpu.SemaphoreType.DMA((2, 2 * nx)),
         ],
         compiler_params=pltpu.CompilerParams(vmem_limit_bytes=56 * 1024 * 1024),
         name="pack",
     )(tokens, grad_out, up_codes, up_scales.T, down_codes, down_scales.T)
 
 
+def weights(ref, feats, sources, blocks):
+    return jnp.concatenate(
+        [
+            jnp.concatenate([ref[s, k * feats : (k + 1) * feats, :] for k in blocks], axis=1)
+            for s in sources
+        ],
+        axis=0,
+    )
+
+
 def forward_kernel(feats, got_ref, out_ref):
     srcs = got_ref.shape[0]
     blocks = out_ref.shape[1] // LANES
-    for k in range(blocks):
+    for k in range(0, blocks, 2):
+        ks = range(k, min(k + 2, blocks))
         total = None
-        for s in range(srcs):
-            part = jnp.dot(
-                got_ref[s, blocks * feats :, :],
-                got_ref[s, k * feats : (k + 1) * feats, :],
-                preferred_element_type=f32,
-            )
+        for s in range(0, srcs, 2):
+            acts = jnp.concatenate([got_ref[s + i, blocks * feats :, :] for i in range(2)], axis=1)
+            part = jnp.dot(acts, weights(got_ref, feats, (s, s + 1), ks), preferred_element_type=f32)
             total = part if total is None else total + part
-        out_ref[:, k * LANES : (k + 1) * LANES] = total.astype(bf16)
+        out_ref[:, k * LANES : (k + len(ks)) * LANES] = total.astype(bf16)
 
 
 def sum_kernel(got_ref, keep_ref, send_ref):
@@ -150,17 +167,19 @@
     core = lax.axis_index("core")
     start = pl.multiple_of((1 - core if theirs else core) * half, half)
     act = act_ref[pl.ds(start, half), :]
-    for s in range(got_ref.shape[0]):
+    for s in range(0, got_ref.shape[0], 2):
         total = None
-        for k in range(blocks):
+        for k in range(0, blocks, 2):
+            ks = range(k, min(k + 2, blocks))
             part = lax.dot_general(
-                act[:, k * LANES : (k + 1) * LANES],
-                got_ref[s, k * feats : (k + 1) * feats, :],
+                act[:, k * LANES : (k + len(ks)) * LANES],
+                weights(got_ref, feats, (s, s + 1), ks),
                 (((1,), (1,)), ((), ())),
                 preferred_element_type=f32,
             )
             total = part if total is None else total + part
-        out_ref[s] = total.astype(out_ref.dtype)
+        for i in range(2):
+            out_ref[s + i] = total[:, i * feats : (i + 1) * feats].astype(out_ref.dtype)
 
 
 def grads_kernel(feats, got_ref, act_ref, out_ref):

time: 138 us -> 137 us (level)
  Pallas kernels: 11 us -> 9.34 us
  transfers between devices with their start and end apart: 7 -> 7, of which waited for: 4 -> 4; matrix products, arithmetic and copies ran while one was open for 0% -> 0% of each run, Pallas kernels for 3% -> 2%
where the time goes in v5:
time: 137 us
  blocking collectives  73.2 us (53%)
  starting transfers between devices  46.2 us (34%)
  Pallas kernels  9.34 us (7%)
  waiting for transfers between devices  6.99 us (5%)
    all_to_all x4, blocking collectives, exchange(): return lax.all_to_all(value, axes, 0, 0, tiled=True)  73.2 us
    ppermute x1, starting transfers between devices, shards(): other = lax.ppermute(send, 'zh', [(0, 1), (1, 0)])  14.9 us
    ppermute x1, starting transfers between devices, shards(): other = lax.ppermute(send, 'core', swap)  8 us
    ppermute x1, starting transfers between devices, shards(): nxt = lax.ppermute(term, 'zl', [(i, (i - 2) % nzl) for i in range(nzl)])  7.77 us
    pallas_call x11, Pallas kernels, call(): pl.pallas_call(kernel, out_shape=out_shape, in_specs=[vmem] * len(args),...  4.87 us
    ppermute x1, starting transfers between devices, shards(): prev = lax.ppermute(term, 'zl', [(i, (i + 2) % nzl) for i in range(nzl)])  4.17 us
    ppermute x1, starting transfers between devices, shards(): lax.ppermute(final, 'core', swap)  4.12 us
    ppermute x1, starting transfers between devices, shards(): other = lax.ppermute(term, 'zl', [(i, i ^ 1) for i in range(nzl)])  3.73 us
  transfers between devices with their start and end apart: 7, of which 4 were waited for; matrix products, arithmetic and copies ran while one was open for 0% of the time, Pallas kernels for 2%

profile of v5, /device:TPU:1, one launch (start us, length us, event | category | flops | bytes accessed | tf_op | source)
XLA Modules:
  0.0 136.6 jit_solution(11992323496339630756)
XLA Ops:
  0.6 3.1 %pack.1 = bf16[8,960,128]{2,1,0:T(8,128)(2,1)} custom-call(bf16[320,128]{1,0:T(8,128)(2,1)} %tok_ref.1, bf16[320,128]{1,0:T(8,128)(2,1)} %grad_ref.1, s32[128,2560]{1,0:T(8,128)} %uc_ref.1, f32[10,128]{1,0:T(8,128)} %bitcast.8, s32[128,2560]{1,0:T(8,128)} %dc_ref.1, f32[10,128]{1,0:T(8,128)} %bitcast.9), custom_call_target="tpu_custom_call" | custom-call | tf_op jit(solution)/shard_map/pack/pallas_call | solution.py:102
  3.7 23.3 %all_to_all.25.got_ref = bf16[8,960,128]{2,1,0:T(8,128)(2,1)S(1)} all-to-all(bf16[8,960,128]{2,1,0:T(8,128)(2,1)} %pack.1), channel_id=1, replica_groups=mesh['x'=4,'yh'=4,'yl'=2,'zh'=2,'zl'=6,'core'=2] {'x','yl'}, dimensions={0} | all-to-all | bytes 3932160 | tf_op jit(solution)/shard_map/all_to_all | solution.py:256
  27.0 0.7 forward.1
  27.7 25.2 %all_to_all.26.got_ref = bf16[8,40,640]{2,1,0:T(8,128)(2,1)S(1)} all-to-all(bf16[8,40,640]{2,1,0:T(8,128)(2,1)S(1)} %bitcast.7), channel_id=1, replica_groups=mesh['x'=4,'yh'=4,'yl'=2,'zh'=2,'zl'=6,'core'=2] {'yh','yl'}, dimensions={0} | all-to-all | bytes 819200 | tf_op jit(solution)/shard_map/all_to_all | solution.py:256
  52.8 0.1 sum.1
  52.9 14.9 %collective-permute-start = (bf16[2,40,640]{2,1,0:T(8,128)(2,1)S(1)}, bf16[2,40,640]{2,1,0:T(8,128)(2,1)S(1)}, u32[]{:S(2)}, u32[]{:S(2)}) collective-permute-start(bf16[2,40,640]{2,1,0:T(8,128)(2,1)S(1)} %get-tuple-element.10), channel_id=1, source_target_pairs={{0,12},{12,0},{1,13},{13,1},{2,14},{14,2},{3,15},{15,3},{4,16},{16... | collective-permute-start | bytes 307208 | tf_op jit(solution)/shard_map/ppermute | solution.py:276
  67.8 2.2 %collective-permute-done.got_ref = bf16[2,40,640]{2,1,0:T(8,128)(2,1)S(1)} collective-permute-done((bf16[2,40,640]{2,1,0:T(8,128)(2,1)S(1)}, bf16[2,40,640]{2,1,0:T(8,128)(2,1)S(1)}, u32[]{:S(2)}, u32[]{:S(2)}) %collective-permute-start) | collective-permute-done | bytes 102432 | tf_op jit(solution)/shard_map/ppermute | solution.py:276
  70.0 0.1 gelu.1
  70.1 14.9 %all_to_all.27 = bf16[8,40,640]{2,1,0:T(8,128)(2,1)S(1)} all-to-all(bf16[8,40,640]{2,1,0:T(8,128)(2,1)S(1)} %gelu.1), channel_id=1, replica_groups=mesh['x'=4,'yh'=4,'yl'=2,'zh'=2,'zl'=6,'core'=2] {'yh','yl'}, dimensions={0} | all-to-all | bytes 819200 | tf_op jit(solution)/shard_map/all_to_all | solution.py:256
  85.0 0.6 terms_send.1
  85.6 8.0 %collective-permute-start.1 = (bf16[8,160,128]{2,1,0:T(8,128)(2,1)S(1)}, bf16[8,160,128]{2,1,0:T(8,128)(2,1)S(1)}, u32[]{:S(2)}, u32[]{:S(2)}) collective-permute-start(bf16[8,160,128]{2,1,0:T(8,128)(2,1)S(1)} %terms_send.1), channel_id=1, source_target_pairs={{0,1},{1,0},{2,3},{3,2},{4,5},{5,4},{6,7},{7,6},{8,9},{9,8},{10,11... | collective-permute-start | bytes 983048 | tf_op jit(solution)/shard_map/ppermute | solution.py:284
  93.6 0.6 terms_keep.1.keep_ref
  94.2 0.7 collective-permute-done.1.got_ref
  94.8 0.1 pair.1
  94.9 9.9 %all_to_all.28.got_ref = bf16[8,160,128]{2,1,0:T(8,128)(2,1)S(1)} all-to-all(bf16[8,160,128]{2,1,0:T(8,128)(2,1)S(1)} %pair.1), channel_id=1, replica_groups=mesh['x'=4,'yh'=4,'yl'=2,'zh'=2,'zl'=6,'core'=2] {'x','yl'}, dimensions={0} | all-to-all | bytes 655360 | tf_op jit(solution)/shard_map/all_to_all | solution.py:256
  104.8 3.7 %collective-permute-start.2 = (f32[160,128]{1,0:T(8,128)S(1)}, f32[160,128]{1,0:T(8,128)S(1)}, u32[]{:S(2)}, u32[]{:S(2)}) collective-permute-start(f32[160,128]{1,0:T(8,128)S(1)} %home.1.keep_ref), channel_id=1, source_target_pairs={{0,2},{2,0},{4,6},{6,4},{8,10},{10,8},{1,3},{3,1},{5,7},{7,5},{9,1... | collective-permute-start | bytes 245768 | tf_op jit(solution)/shard_map/ppermute | solution.py:291
  108.6 2.1 %grads.1 = bf16[8,640,128]{2,1,0:T(8,128)(2,1)} custom-call(bf16[8,960,128]{2,1,0:T(8,128)(2,1)S(1)} %all_to_all.25.got_ref, bf16[320,640]{1,0:T(8,128)(2,1)S(1)} %bitcast.6), custom_call_target="tpu_custom_call" | custom-call | tf_op jit(solution)/shard_map/grads/pallas_call | solution.py:31
  110.7 0.0 collective-permute-done.2.got_ref
  110.7 3.6 %all-to-all-start.4 = ((bf16[8,640,128]{2,1,0:T(8,128)(2,1)}), bf16[8,640,128]{2,1,0:T(8,128)(2,1)S(1)}, u32[]{:S(2)}, u32[]{:S(2)}) async-start(bf16[8,640,128]{2,1,0:T(8,128)(2,1)} %grads.1), calls=%async_computation.4 | async-start | bytes 2621440 | tf_op jit(solution)/shard_map/all_to_all | solution.py:256
  114.3 4.2 %collective-permute-start.3 = (bf16[160,128]{1,0:T(8,128)(2,1)S(1)}, bf16[160,128]{1,0:T(8,128)(2,1)S(1)}, u32[]{:S(2)}, u32[]{:S(2)}) collective-permute-start(bf16[160,128]{1,0:T(8,128)(2,1)S(1)} %pairs.1.own_ref), channel_id=1, source_target_pairs={{0,4},{2,6},{4,8},{6,10},{8,0},{10,2},{1,5},{3,7},{5,9},{7,11},{9,... | collective-permute-start | bytes 122888 | tf_op jit(solution)/shard_map/ppermute | solution.py:295
  118.5 7.8 %collective-permute-start.4 = (bf16[160,128]{1,0:T(8,128)(2,1)S(1)}, bf16[160,128]{1,0:T(8,128)(2,1)S(1)}, u32[]{:S(2)}, u32[]{:S(2)}) collective-permute-start(bf16[160,128]{1,0:T(8,128)(2,1)S(1)} %pairs.1.own_ref), channel_id=1, source_target_pairs={{0,8},{2,10},{4,0},{6,2},{8,4},{10,6},{1,9},{3,11},{5,1},{7,3},{9,... | collective-permute-start | bytes 122888 | tf_op jit(solution)/shard_map/ppermute | solution.py:296
  126.2 0.0 collective-permute-done.3.prev_ref
  126.2 3.2 %collective-permute-done.4.next_ref = bf16[160,128]{1,0:T(8,128)(2,1)S(1)} collective-permute-done((bf16[160,128]{1,0:T(8,128)(2,1)S(1)}, bf16[160,128]{1,0:T(8,128)(2,1)S(1)}, u32[]{:S(2)}, u32[]{:S(2)}) %collective-permute-start.4) | collective-permute-done | bytes 40992 | tf_op jit(solution)/shard_map/ppermute | solution.py:296
  129.5 4.1 %collective-permute-start.5 = (bf16[160,128]{1,0:T(8,128)(2,1)S(1)}, bf16[160,128]{1,0:T(8,128)(2,1)S(1)}, u32[]{:S(2)}, u32[]{:S(2)}) collective-permute-start(bf16[160,128]{1,0:T(8,128)(2,1)S(1)} %triples.1.own_ref), channel_id=1, source_target_pairs={{0,1},{1,0},{2,3},{3,2},{4,5},{5,4},{6,7},{7,6},{8,9},{9,8},{10,11... | collective-permute-start | bytes 122888 | tf_op jit(solution)/shard_map/ppermute | solution.py:299
  133.7 0.8 collective-permute-done.5.other_ref
  134.5 0.6 halves.1
  135.2 0.0 all-to-all-done.4.got_ref
  135.2 1.4 %unpack.1 = (bf16[128,2560]{1,0:T(8,128)(2,1)}, bf16[128,2560]{1,0:T(8,128)(2,1)}) custom-call(bf16[8,640,128]{2,1,0:T(8,128)(2,1)S(1)} %all-to-all-done.4.got_ref), custom_call_target="tpu_custom_call" | custom-call | tf_op jit(solution)/shard_map/unpack/pallas_call | solution.py:244
  (3 shorter events, 0.1 us)
Async XLA Ops:
  52.9 17.1 %collective-permute-start = (bf16[2,40,640]{2,1,0:T(8,128)(2,1)S(1)}, bf16[2,40,640]{2,1,0:T(8,128)(2,1)S(1)}, u32[]{:S(2)}, u32[]{:S(2)}) collective-permute-start(bf16[2,40,640]{2,1,0:T(8,128)(2,1)S(1)} %get-tuple-element.10), channel_id=1, source_target_pairs={{0,12},{12,0},{1,13},{13,1},{2,14},{14,2},{3,15},{15,3},{4,16},{16... | collective-permute-start | bytes 307208 | tf_op jit(solution)/shard_map/ppermute | solution.py:276
  85.6 9.2 %collective-permute-start.1 = (bf16[8,160,128]{2,1,0:T(8,128)(2,1)S(1)}, bf16[8,160,128]{2,1,0:T(8,128)(2,1)S(1)}, u32[]{:S(2)}, u32[]{:S(2)}) collective-permute-start(bf16[8,160,128]{2,1,0:T(8,128)(2,1)S(1)} %terms_send.1), channel_id=1, source_target_pairs={{0,1},{1,0},{2,3},{3,2},{4,5},{5,4},{6,7},{7,6},{8,9},{9,8},{10,11... | collective-permute-start | bytes 983048 | tf_op jit(solution)/shard_map/ppermute | solution.py:284
  104.8 5.9 %collective-permute-start.2 = (f32[160,128]{1,0:T(8,128)S(1)}, f32[160,128]{1,0:T(8,128)S(1)}, u32[]{:S(2)}, u32[]{:S(2)}) collective-permute-start(f32[160,128]{1,0:T(8,128)S(1)} %home.1.keep_ref), channel_id=1, source_target_pairs={{0,2},{2,0},{4,6},{6,4},{8,10},{10,8},{1,3},{3,1},{5,7},{7,5},{9,1... | collective-permute-start | bytes 245768 | tf_op jit(solution)/shard_map/ppermute | solution.py:291
  110.7 24.5 %all-to-all-start.4 = ((bf16[8,640,128]{2,1,0:T(8,128)(2,1)}), bf16[8,640,128]{2,1,0:T(8,128)(2,1)S(1)}, u32[]{:S(2)}, u32[]{:S(2)}) async-start(bf16[8,640,128]{2,1,0:T(8,128)(2,1)} %grads.1), calls=%async_computation.4 | async-start | bytes 2621440 | tf_op jit(solution)/shard_map/all_to_all | solution.py:256
  114.3 12.0 %collective-permute-start.3 = (bf16[160,128]{1,0:T(8,128)(2,1)S(1)}, bf16[160,128]{1,0:T(8,128)(2,1)S(1)}, u32[]{:S(2)}, u32[]{:S(2)}) collective-permute-start(bf16[160,128]{1,0:T(8,128)(2,1)S(1)} %pairs.1.own_ref), channel_id=1, source_target_pairs={{0,4},{2,6},{4,8},{6,10},{8,0},{10,2},{1,5},{3,7},{5,9},{7,11},{9,... | collective-permute-start | bytes 122888 | tf_op jit(solution)/shard_map/ppermute | solution.py:295
  118.5 11.0 %collective-permute-start.4 = (bf16[160,128]{1,0:T(8,128)(2,1)S(1)}, bf16[160,128]{1,0:T(8,128)(2,1)S(1)}, u32[]{:S(2)}, u32[]{:S(2)}) collective-permute-start(bf16[160,128]{1,0:T(8,128)(2,1)S(1)} %pairs.1.own_ref), channel_id=1, source_target_pairs={{0,8},{2,10},{4,0},{6,2},{8,4},{10,6},{1,9},{3,11},{5,1},{7,3},{9,... | collective-permute-start | bytes 122888 | tf_op jit(solution)/shard_map/ppermute | solution.py:296
  129.5 5.0 %collective-permute-start.5 = (bf16[160,128]{1,0:T(8,128)(2,1)S(1)}, bf16[160,128]{1,0:T(8,128)(2,1)S(1)}, u32[]{:S(2)}, u32[]{:S(2)}) collective-permute-start(bf16[160,128]{1,0:T(8,128)(2,1)S(1)} %triples.1.own_ref), channel_id=1, source_target_pairs={{0,1},{1,0},{2,3},{3,2},{4,5},{5,4},{6,7},{7,6},{8,9},{9,8},{10,11... | collective-permute-start | bytes 122888 | tf_op jit(solution)/shard_map/ppermute | solution.py:299

commit v6 on v5

--- a/solution.py
+++ b/solution.py
@@ -286,19 +286,19 @@
     keep = call(
         functools.partial(terms_kernel, feats, False), S((srcs, half, feats), f32), got, act, name="terms_keep"
     )
+    other, grads = lax.optimization_barrier((other, grads))
     terms = exchange(call(pair_kernel, S((srcs, half, feats), bf16), keep, other, name="pair"), ("x", "yl"))
     term = call(home_kernel, S((half, feats), f32), terms, name="home")
+    term, grads = lax.optimization_barrier((term, grads))
+    grad_up, grad_down = unpack(feats, units, exchange(grads, ("x", "yl")))
     other = lax.ppermute(term, "zl", [(i, i ^ 1) for i in range(nzl)])
     term = call(pair_kernel, S((half, feats), bf16), term, other, name="pairs")
-    term, grads = lax.optimization_barrier((term, grads))
-    home = exchange(grads, ("x", "yl"))
     prev = lax.ppermute(term, "zl", [(i, (i + 2) % nzl) for i in range(nzl)])
     nxt = lax.ppermute(term, "zl", [(i, (i - 2) % nzl) for i in range(nzl)])
     final = call(triple_kernel, S((half, feats), bf16), term, prev, nxt, name="triples")
-    grad_tokens = call(
-        halves_kernel, S((tok, feats), bf16), final, lax.ppermute(final, "core", swap), name="halves"
-    )
-    grad_up, grad_down = unpack(feats, units, home)
+    other = lax.ppermute(final, "core", swap)
+    other, grad_up, grad_down = lax.optimization_barrier((other, grad_up, grad_down))
+    grad_tokens = call(halves_kernel, S((tok, feats), bf16), final, other, name="halves")
     return grad_up, grad_down, grad_tokens
 
 

time: 137 us -> 143 us (1.044)
  waiting for transfers between devices: 6.99 us -> 11.2 us
    ppermute x1, waiting for transfers between devices: 0.01 us -> 6.88 us  [shards(): prev = lax.ppermute(term, 'zl', [(i, (i + 2) % nzl) for i in range(nzl)])]
    ppermute x1, waiting for transfers between devices: 3.25 us -> 0.01 us  [shards(): nxt = lax.ppermute(term, 'zl', [(i, (i - 2) % nzl) for i in range(nzl)])]
    ppermute x1, starting transfers between devices: 7.77 us -> 10.3 us  [shards(): nxt = lax.ppermute(term, 'zl', [(i, (i - 2) % nzl) for i in range(nzl)])]
    ppermute x1, starting transfers between devices: 4.17 us -> 1.92 us  [shards(): prev = lax.ppermute(term, 'zl', [(i, (i + 2) % nzl) for i in range(nzl)])]
    ppermute x1, waiting for transfers between devices: 0.01 us -> 2.11 us  [shards(): other = lax.ppermute(term, 'zl', [(i, i ^ 1) for i in range(nzl)])]
  transfers between devices with their start and end apart: 7 -> 7, of which waited for: 4 -> 3; matrix products, arithmetic and copies ran while one was open for 0% -> 0% of each run, Pallas kernels for 2% -> 3%
where the time goes in v6:
time: 143 us
  blocking collectives  73.9 us (52%)
  starting transfers between devices  47.3 us (33%)
  waiting for transfers between devices  11.2 us (8%)
  Pallas kernels  9.36 us (7%)
    all_to_all x4, blocking collectives, exchange(): return lax.all_to_all(value, axes, 0, 0, tiled=True)  73.9 us
    ppermute x1, starting transfers between devices, shards(): other = lax.ppermute(send, 'zh', [(0, 1), (1, 0)])  14.9 us
    ppermute x1, starting transfers between devices, shards(): nxt = lax.ppermute(term, 'zl', [(i, (i - 2) % nzl) for i in range(nzl)])  10.3 us
    ppermute x1, starting transfers between devices, shards(): other = lax.ppermute(send, 'core', swap)  8 us
    ppermute x1, waiting for transfers between devices, shards(): prev = lax.ppermute(term, 'zl', [(i, (i + 2) % nzl) for i in range(nzl)])  6.88 us
    ppermute x1, starting transfers between devices, shards(): other = lax.ppermute(final, 'core', swap)  4.93 us
    pallas_call x11, Pallas kernels, call(): pl.pallas_call(kernel, out_shape=out_shape, in_specs=[vmem] * len(args),...  4.88 us
    ppermute x1, starting transfers between devices, shards(): other = lax.ppermute(term, 'zl', [(i, i ^ 1) for i in range(nzl)])  3.73 us
  transfers between devices with their start and end apart: 7, of which 3 were waited for; matrix products, arithmetic and copies ran while one was open for 0% of the time, Pallas kernels for 3%

profile of v6, /device:TPU:1, one launch (start us, length us, event | category | flops | bytes accessed | tf_op | source)
XLA Modules:
  0.0 142.6 jit_solution(11977052463889413193)
XLA Ops:
  0.6 3.1 %pack.1 = bf16[8,960,128]{2,1,0:T(8,128)(2,1)} custom-call(bf16[320,128]{1,0:T(8,128)(2,1)} %tok_ref.1, bf16[320,128]{1,0:T(8,128)(2,1)} %grad_ref.1, s32[128,2560]{1,0:T(8,128)} %uc_ref.1, f32[10,128]{1,0:T(8,128)} %bitcast.8, s32[128,2560]{1,0:T(8,128)} %dc_ref.1, f32[10,128]{1,0:T(8,128)} %bitcast.9), custom_call_target="tpu_custom_call" | custom-call | tf_op jit(solution)/shard_map/pack/pallas_call | solution.py:102
  3.7 23.3 %all_to_all.25.got_ref = bf16[8,960,128]{2,1,0:T(8,128)(2,1)S(1)} all-to-all(bf16[8,960,128]{2,1,0:T(8,128)(2,1)} %pack.1), channel_id=1, replica_groups=mesh['x'=4,'yh'=4,'yl'=2,'zh'=2,'zl'=6,'core'=2] {'x','yl'}, dimensions={0} | all-to-all | bytes 3932160 | tf_op jit(solution)/shard_map/all_to_all | solution.py:256
  27.0 0.7 forward.1
  27.7 25.2 %all_to_all.26.got_ref = bf16[8,40,640]{2,1,0:T(8,128)(2,1)S(1)} all-to-all(bf16[8,40,640]{2,1,0:T(8,128)(2,1)S(1)} %bitcast.7), channel_id=1, replica_groups=mesh['x'=4,'yh'=4,'yl'=2,'zh'=2,'zl'=6,'core'=2] {'yh','yl'}, dimensions={0} | all-to-all | bytes 819200 | tf_op jit(solution)/shard_map/all_to_all | solution.py:256
  52.8 0.1 sum.1
  52.9 14.9 %collective-permute-start = (bf16[2,40,640]{2,1,0:T(8,128)(2,1)S(1)}, bf16[2,40,640]{2,1,0:T(8,128)(2,1)S(1)}, u32[]{:S(2)}, u32[]{:S(2)}) collective-permute-start(bf16[2,40,640]{2,1,0:T(8,128)(2,1)S(1)} %get-tuple-element.15), channel_id=1, source_target_pairs={{0,12},{12,0},{1,13},{13,1},{2,14},{14,2},{3,15},{15,3},{4,16},{16... | collective-permute-start | bytes 307208 | tf_op jit(solution)/shard_map/ppermute | solution.py:276
  67.8 2.2 %collective-permute-done.got_ref = bf16[2,40,640]{2,1,0:T(8,128)(2,1)S(1)} collective-permute-done((bf16[2,40,640]{2,1,0:T(8,128)(2,1)S(1)}, bf16[2,40,640]{2,1,0:T(8,128)(2,1)S(1)}, u32[]{:S(2)}, u32[]{:S(2)}) %collective-permute-start) | collective-permute-done | bytes 102432 | tf_op jit(solution)/shard_map/ppermute | solution.py:276
  70.0 0.1 gelu.1
  70.1 14.9 %all_to_all.27 = bf16[8,40,640]{2,1,0:T(8,128)(2,1)S(1)} all-to-all(bf16[8,40,640]{2,1,0:T(8,128)(2,1)S(1)} %gelu.1), channel_id=1, replica_groups=mesh['x'=4,'yh'=4,'yl'=2,'zh'=2,'zl'=6,'core'=2] {'yh','yl'}, dimensions={0} | all-to-all | bytes 819200 | tf_op jit(solution)/shard_map/all_to_all | solution.py:256
  85.0 0.6 terms_send.1
  85.6 8.0 %collective-permute-start.1 = (bf16[8,160,128]{2,1,0:T(8,128)(2,1)S(1)}, bf16[8,160,128]{2,1,0:T(8,128)(2,1)S(1)}, u32[]{:S(2)}, u32[]{:S(2)}) collective-permute-start(bf16[8,160,128]{2,1,0:T(8,128)(2,1)S(1)} %terms_send.1), channel_id=1, source_target_pairs={{0,1},{1,0},{2,3},{3,2},{4,5},{5,4},{6,7},{7,6},{8,9},{9,8},{10,11... | collective-permute-start | bytes 983048 | tf_op jit(solution)/shard_map/ppermute | solution.py:284
  93.6 0.6 terms_keep.1.keep_ref
  94.2 2.1 %grads.1 = bf16[8,640,128]{2,1,0:T(8,128)(2,1)} custom-call(bf16[8,960,128]{2,1,0:T(8,128)(2,1)S(1)} %all_to_all.25.got_ref, bf16[320,640]{1,0:T(8,128)(2,1)S(1)} %bitcast.6), custom_call_target="tpu_custom_call" | custom-call | tf_op jit(solution)/shard_map/grads/pallas_call | solution.py:31
  96.3 0.0 collective-permute-done.1.got_ref
  96.3 0.1 pair.1
  96.4 10.5 %all_to_all.28.got_ref = bf16[8,160,128]{2,1,0:T(8,128)(2,1)S(1)} all-to-all(bf16[8,160,128]{2,1,0:T(8,128)(2,1)S(1)} %pair.1), channel_id=1, replica_groups=mesh['x'=4,'yh'=4,'yl'=2,'zh'=2,'zl'=6,'core'=2] {'x','yl'}, dimensions={0} | all-to-all | bytes 655360 | tf_op jit(solution)/shard_map/all_to_all | solution.py:256
  106.9 3.6 %all-to-all-start.4 = ((bf16[8,640,128]{2,1,0:T(8,128)(2,1)}), bf16[8,640,128]{2,1,0:T(8,128)(2,1)S(1)}, u32[]{:S(2)}, u32[]{:S(2)}) async-start(bf16[8,640,128]{2,1,0:T(8,128)(2,1)} %grads.1), calls=%async_computation.4 | async-start | bytes 2621440 | tf_op jit(solution)/shard_map/all_to_all | solution.py:256
  110.5 3.7 %collective-permute-start.2 = (f32[160,128]{1,0:T(8,128)S(1)}, f32[160,128]{1,0:T(8,128)S(1)}, u32[]{:S(2)}, u32[]{:S(2)}) collective-permute-start(f32[160,128]{1,0:T(8,128)S(1)} %home.1.keep_ref), channel_id=1, source_target_pairs={{0,2},{2,0},{4,6},{6,4},{8,10},{10,8},{1,3},{3,1},{5,7},{7,5},{9,1... | collective-permute-start | bytes 245768 | tf_op jit(solution)/shard_map/ppermute | solution.py:294
  114.2 2.1 %collective-permute-done.2.got_ref = f32[160,128]{1,0:T(8,128)S(1)} collective-permute-done((f32[160,128]{1,0:T(8,128)S(1)}, f32[160,128]{1,0:T(8,128)S(1)}, u32[]{:S(2)}, u32[]{:S(2)}) %collective-permute-start.2) | collective-permute-done | bytes 81952 | tf_op jit(solution)/shard_map/ppermute | solution.py:294
  116.4 10.3 %collective-permute-start.4 = (bf16[160,128]{1,0:T(8,128)(2,1)S(1)}, bf16[160,128]{1,0:T(8,128)(2,1)S(1)}, u32[]{:S(2)}, u32[]{:S(2)}) collective-permute-start(bf16[160,128]{1,0:T(8,128)(2,1)S(1)} %pairs.1.own_ref), channel_id=1, source_target_pairs={{0,8},{2,10},{4,0},{6,2},{8,4},{10,6},{1,9},{3,11},{5,1},{7,3},{9,... | collective-permute-start | bytes 122888 | tf_op jit(solution)/shard_map/ppermute | solution.py:297
  126.7 1.9 %collective-permute-start.3 = (bf16[160,128]{1,0:T(8,128)(2,1)S(1)}, bf16[160,128]{1,0:T(8,128)(2,1)S(1)}, u32[]{:S(2)}, u32[]{:S(2)}) collective-permute-start(bf16[160,128]{1,0:T(8,128)(2,1)S(1)} %pairs.1.own_ref), channel_id=1, source_target_pairs={{0,4},{2,6},{4,8},{6,10},{8,0},{10,2},{1,5},{3,7},{5,9},{7,11},{9,... | collective-permute-start | bytes 122888 | tf_op jit(solution)/shard_map/ppermute | solution.py:296
  128.6 0.0 collective-permute-done.4.next_ref
  128.6 6.9 %collective-permute-done.3.prev_ref = bf16[160,128]{1,0:T(8,128)(2,1)S(1)} collective-permute-done((bf16[160,128]{1,0:T(8,128)(2,1)S(1)}, bf16[160,128]{1,0:T(8,128)(2,1)S(1)}, u32[]{:S(2)}, u32[]{:S(2)}) %collective-permute-start.3) | collective-permute-done | bytes 40992 | tf_op jit(solution)/shard_map/ppermute | solution.py:296
  135.6 4.9 %collective-permute-start.5 = (bf16[160,128]{1,0:T(8,128)(2,1)S(1)}, bf16[160,128]{1,0:T(8,128)(2,1)S(1)}, u32[]{:S(2)}, u32[]{:S(2)}) collective-permute-start(bf16[160,128]{1,0:T(8,128)(2,1)S(1)} %triples.1.own_ref), channel_id=1, source_target_pairs={{0,1},{1,0},{2,3},{3,2},{4,5},{5,4},{6,7},{7,6},{8,9},{9,8},{10,11... | collective-permute-start | bytes 122888 | tf_op jit(solution)/shard_map/ppermute | solution.py:299
  140.5 0.0 all-to-all-done.4.got_ref
  140.5 1.4 unpack.1
  141.9 0.0 collective-permute-done.5.other_ref
  141.9 0.7 halves.1
  (3 shorter events, 0.1 us)
Async XLA Ops:
  52.9 17.1 %collective-permute-start = (bf16[2,40,640]{2,1,0:T(8,128)(2,1)S(1)}, bf16[2,40,640]{2,1,0:T(8,128)(2,1)S(1)}, u32[]{:S(2)}, u32[]{:S(2)}) collective-permute-start(bf16[2,40,640]{2,1,0:T(8,128)(2,1)S(1)} %get-tuple-element.15), channel_id=1, source_target_pairs={{0,12},{12,0},{1,13},{13,1},{2,14},{14,2},{3,15},{15,3},{4,16},{16... | collective-permute-start | bytes 307208 | tf_op jit(solution)/shard_map/ppermute | solution.py:276
  85.6 10.7 %collective-permute-start.1 = (bf16[8,160,128]{2,1,0:T(8,128)(2,1)S(1)}, bf16[8,160,128]{2,1,0:T(8,128)(2,1)S(1)}, u32[]{:S(2)}, u32[]{:S(2)}) collective-permute-start(bf16[8,160,128]{2,1,0:T(8,128)(2,1)S(1)} %terms_send.1), channel_id=1, source_target_pairs={{0,1},{1,0},{2,3},{3,2},{4,5},{5,4},{6,7},{7,6},{8,9},{9,8},{10,11... | collective-permute-start | bytes 983048 | tf_op jit(solution)/shard_map/ppermute | solution.py:284
  106.9 33.6 %all-to-all-start.4 = ((bf16[8,640,128]{2,1,0:T(8,128)(2,1)}), bf16[8,640,128]{2,1,0:T(8,128)(2,1)S(1)}, u32[]{:S(2)}, u32[]{:S(2)}) async-start(bf16[8,640,128]{2,1,0:T(8,128)(2,1)} %grads.1), calls=%async_computation.4 | async-start | bytes 2621440 | tf_op jit(solution)/shard_map/all_to_all | solution.py:256
  110.5 5.8 %collective-permute-start.2 = (f32[160,128]{1,0:T(8,128)S(1)}, f32[160,128]{1,0:T(8,128)S(1)}, u32[]{:S(2)}, u32[]{:S(2)}) collective-permute-start(f32[160,128]{1,0:T(8,128)S(1)} %home.1.keep_ref), channel_id=1, source_target_pairs={{0,2},{2,0},{4,6},{6,4},{8,10},{10,8},{1,3},{3,1},{5,7},{7,5},{9,1... | collective-permute-start | bytes 245768 | tf_op jit(solution)/shard_map/ppermute | solution.py:294
  116.4 12.3 %collective-permute-start.4 = (bf16[160,128]{1,0:T(8,128)(2,1)S(1)}, bf16[160,128]{1,0:T(8,128)(2,1)S(1)}, u32[]{:S(2)}, u32[]{:S(2)}) collective-permute-start(bf16[160,128]{1,0:T(8,128)(2,1)S(1)} %pairs.1.own_ref), channel_id=1, source_target_pairs={{0,8},{2,10},{4,0},{6,2},{8,4},{10,6},{1,9},{3,11},{5,1},{7,3},{9,... | collective-permute-start | bytes 122888 | tf_op jit(solution)/shard_map/ppermute | solution.py:297
  126.7 8.8 %collective-permute-start.3 = (bf16[160,128]{1,0:T(8,128)(2,1)S(1)}, bf16[160,128]{1,0:T(8,128)(2,1)S(1)}, u32[]{:S(2)}, u32[]{:S(2)}) collective-permute-start(bf16[160,128]{1,0:T(8,128)(2,1)S(1)} %pairs.1.own_ref), channel_id=1, source_target_pairs={{0,4},{2,6},{4,8},{6,10},{8,0},{10,2},{1,5},{3,7},{5,9},{7,11},{9,... | collective-permute-start | bytes 122888 | tf_op jit(solution)/shard_map/ppermute | solution.py:296
  135.6 6.3 %collective-permute-start.5 = (bf16[160,128]{1,0:T(8,128)(2,1)S(1)}, bf16[160,128]{1,0:T(8,128)(2,1)S(1)}, u32[]{:S(2)}, u32[]{:S(2)}) collective-permute-start(bf16[160,128]{1,0:T(8,128)(2,1)S(1)} %triples.1.own_ref), channel_id=1, source_target_pairs={{0,1},{1,0},{2,3},{3,2},{4,5},{5,4},{6,7},{7,6},{8,9},{9,8},{10,11... | collective-permute-start | bytes 122888 | tf_op jit(solution)/shard_map/ppermute | solution.py:299

commit v7 on v5

--- a/solution.py
+++ b/solution.py
@@ -200,23 +200,16 @@
     total = got_ref[0].astype(f32)
     for x in range(1, got_ref.shape[0] // 2):
         total = total + got_ref[2 * x].astype(f32)
-    out_ref[...] = total
-
-
-def triple_kernel(own_ref, prev_ref, next_ref, out_ref):
-    pos = lax.div(lax.axis_index("zl"), 2)
-    own, prev, nxt = (r[...].astype(f32) for r in (own_ref, prev_ref, next_ref))
-    first = jnp.where(pos == 0, own, jnp.where(pos == 1, prev, nxt))
-    second = jnp.where(pos == 1, own, jnp.where(pos == 2, prev, nxt))
-    third = jnp.where(pos == 2, own, jnp.where(pos == 0, prev, nxt))
-    out_ref[...] = (first + second + third).astype(bf16)
-
-
-def halves_kernel(own_ref, other_ref, out_ref):
-    half = own_ref.shape[0]
-    core = lax.axis_index("core")
-    out_ref[pl.ds(pl.multiple_of(core * half, half), half), :] = own_ref[...]
-    out_ref[pl.ds(pl.multiple_of((1 - core) * half, half), half), :] = other_ref[...]
+    out_ref[...] = total.astype(bf16)
+
+
+def reduce_kernel(got_ref, out_ref):
+    half = got_ref.shape[1]
+    for c in range(2):
+        total = got_ref[c].astype(f32)
+        for z in range(1, got_ref.shape[0] // 2):
+            total = total + got_ref[2 * z + c].astype(f32)
+        out_ref[c * half : (c + 1) * half, :] = total.astype(bf16)
 
 
 def unpack_kernel(feats, got_ref, up_ref, down_ref, sems):
@@ -257,7 +250,7 @@
 
 
 def shards(sizes, tokens, grad_out, up_codes, up_scales, down_codes, down_scales):
-    nx, nyh, nyl, nzl, ncore = (sizes[a] for a in ("x", "yh", "yl", "zl", "core"))
+    nx, nyh, nyl, ncore = (sizes[a] for a in ("x", "yh", "yl", "core"))
     feats, units = up_codes.shape
     tok = tokens.shape[0]
     mine = units // nx
@@ -287,17 +280,11 @@
         functools.partial(terms_kernel, feats, False), S((srcs, half, feats), f32), got, act, name="terms_keep"
     )
     terms = exchange(call(pair_kernel, S((srcs, half, feats), bf16), keep, other, name="pair"), ("x", "yl"))
-    term = call(home_kernel, S((half, feats), f32), terms, name="home")
-    other = lax.ppermute(term, "zl", [(i, i ^ 1) for i in range(nzl)])
-    term = call(pair_kernel, S((half, feats), bf16), term, other, name="pairs")
+    term = call(home_kernel, S((half, feats), bf16), terms, name="home")
     term, grads = lax.optimization_barrier((term, grads))
     home = exchange(grads, ("x", "yl"))
-    prev = lax.ppermute(term, "zl", [(i, (i + 2) % nzl) for i in range(nzl)])
-    nxt = lax.ppermute(term, "zl", [(i, (i - 2) % nzl) for i in range(nzl)])
-    final = call(triple_kernel, S((half, feats), bf16), term, prev, nxt, name="triples")
-    grad_tokens = call(
-        halves_kernel, S((tok, feats), bf16), final, lax.ppermute(final, "core", swap), name="halves"
-    )
+    halves = lax.all_gather(term, ("zl", "core"), axis=0, tiled=False)
+    grad_tokens = call(reduce_kernel, S((tok, feats), bf16), halves, name="reduce")
     grad_up, grad_down = unpack(feats, units, home)
     return grad_up, grad_down, grad_tokens
 

time: 137 us -> 139 us (1.015)
  blocking collectives: 73.2 us -> 89.7 us
  starting transfers between devices: 46.2 us -> 29.9 us
  waiting for transfers between devices: 6.99 us -> 8.44 us
    all_gather x0 -> x1, blocking collectives: none -> 26.4 us  [shards(): halves = lax.all_gather(term, ('zl', 'core'), axis=0, tiled=False)]
    ppermute x4 -> x0, starting transfers between devices: 19.8 us -> none  [the longest x1 7.77 us: shards(): nxt = lax.ppermute(term, 'zl', [(i, (i - 2) % nzl) for i in range(nzl)])]
    all_to_all x4 -> x3, blocking collectives: 73.2 us -> 63.3 us  [exchange(): return lax.all_to_all(value, axes, 0, 0, tiled=True)]
    all_to_all x1 -> x2, waiting for transfers between devices: 0.01 us -> 5.56 us  [exchange(): return lax.all_to_all(value, axes, 0, 0, tiled=True)]
    ppermute x4 -> x0, waiting for transfers between devices: 4.1 us -> none  [the longest x1 3.25 us: shards(): nxt = lax.ppermute(term, 'zl', [(i, (i - 2) % nzl) for i in range(nzl)])]
    all_to_all x1 -> x2, starting transfers between devices: 3.58 us -> 7.01 us  [exchange(): return lax.all_to_all(value, axes, 0, 0, tiled=True)]
    pallas_call x11 -> x9, Pallas kernels: 4.87 us -> 4.51 us  [call(): pl.pallas_call(kernel, out_shape=out_shape, in_specs=[vmem] * len(args),...]
  transfers between devices with their start and end apart: 7 -> 4, of which waited for: 4 -> 3; matrix products, arithmetic and copies ran while one was open for 0% -> 0% of each run, Pallas kernels for 2% -> 2%
where the time goes in v7:
time: 139 us
  blocking collectives  89.7 us (65%)
  starting transfers between devices  29.9 us (22%)
  Pallas kernels  8.97 us (6%)
  waiting for transfers between devices  8.44 us (6%)
    all_to_all x3, blocking collectives, exchange(): return lax.all_to_all(value, axes, 0, 0, tiled=True)  63.3 us
    all_gather x1, blocking collectives, shards(): halves = lax.all_gather(term, ('zl', 'core'), axis=0, tiled=False)  26.4 us
    ppermute x1, starting transfers between devices, shards(): other = lax.ppermute(send, 'zh', [(0, 1), (1, 0)])  14.9 us
    ppermute x1, starting transfers between devices, shards(): other = lax.ppermute(send, 'core', swap)  7.99 us
    all_to_all x2, starting transfers between devices, exchange(): return lax.all_to_all(value, axes, 0, 0, tiled=True)  7.01 us
    all_to_all x2, waiting for transfers between devices, exchange(): return lax.all_to_all(value, axes, 0, 0, tiled=True)  5.56 us
    pallas_call x9, Pallas kernels, call(): pl.pallas_call(kernel, out_shape=out_shape, in_specs=[vmem] * len(args),...  4.51 us
    pallas_call x1, Pallas kernels, pack(): pl.pallas_call(functools.partial(pack_kernel, nx), out_shape=jax.ShapeDty...  3.07 us
  transfers between devices with their start and end apart: 4, of which 3 were waited for; matrix products, arithmetic and copies ran while one was open for 0% of the time, Pallas kernels for 2%

profile of v7, /device:TPU:1, one launch (start us, length us, event | category | flops | bytes accessed | tf_op | source)
XLA Modules:
  0.0 138.8 jit_solution(4982240623952704527)
XLA Ops:
  0.6 3.1 %pack.1 = bf16[8,960,128]{2,1,0:T(8,128)(2,1)} custom-call(bf16[320,128]{1,0:T(8,128)(2,1)} %tok_ref.1, bf16[320,128]{1,0:T(8,128)(2,1)} %grad_ref.1, s32[128,2560]{1,0:T(8,128)} %uc_ref.1, f32[10,128]{1,0:T(8,128)} %bitcast.10, s32[128,2560]{1,0:T(8,128)} %dc_ref.1, f32[10,128]{1,0:T(8,128)} %bitcast.11), custom_call_target="tpu_custom_call" | custom-call | tf_op jit(solution)/shard_map/pack/pallas_call | solution.py:102
  3.7 23.3 %all_to_all.25.got_ref = bf16[8,960,128]{2,1,0:T(8,128)(2,1)S(1)} all-to-all(bf16[8,960,128]{2,1,0:T(8,128)(2,1)} %pack.1), channel_id=1, replica_groups=mesh['x'=4,'yh'=4,'yl'=2,'zh'=2,'zl'=6,'core'=2] {'x','yl'}, dimensions={0} | all-to-all | bytes 3932160 | tf_op jit(solution)/shard_map/all_to_all | solution.py:249
  27.0 0.7 forward.1
  27.7 25.2 %all_to_all.26.got_ref = bf16[8,40,640]{2,1,0:T(8,128)(2,1)S(1)} all-to-all(bf16[8,40,640]{2,1,0:T(8,128)(2,1)S(1)} %bitcast.9), channel_id=1, replica_groups=mesh['x'=4,'yh'=4,'yl'=2,'zh'=2,'zl'=6,'core'=2] {'yh','yl'}, dimensions={0} | all-to-all | bytes 819200 | tf_op jit(solution)/shard_map/all_to_all | solution.py:249
  52.8 0.1 sum.1
  52.9 14.9 %collective-permute-start = (bf16[2,40,640]{2,1,0:T(8,128)(2,1)S(1)}, bf16[2,40,640]{2,1,0:T(8,128)(2,1)S(1)}, u32[]{:S(2)}, u32[]{:S(2)}) collective-permute-start(bf16[2,40,640]{2,1,0:T(8,128)(2,1)S(1)} %get-tuple-element.10), channel_id=1, source_target_pairs={{0,12},{12,0},{1,13},{13,1},{2,14},{14,2},{3,15},{15,3},{4,16},{16... | collective-permute-start | bytes 307208 | tf_op jit(solution)/shard_map/ppermute | solution.py:269
  67.8 2.2 %collective-permute-done.got_ref = bf16[2,40,640]{2,1,0:T(8,128)(2,1)S(1)} collective-permute-done((bf16[2,40,640]{2,1,0:T(8,128)(2,1)S(1)}, bf16[2,40,640]{2,1,0:T(8,128)(2,1)S(1)}, u32[]{:S(2)}, u32[]{:S(2)}) %collective-permute-start) | collective-permute-done | bytes 102432 | tf_op jit(solution)/shard_map/ppermute | solution.py:269
  70.0 0.1 gelu.1
  70.1 14.9 %all_to_all.27 = bf16[8,40,640]{2,1,0:T(8,128)(2,1)S(1)} all-to-all(bf16[8,40,640]{2,1,0:T(8,128)(2,1)S(1)} %gelu.1), channel_id=1, replica_groups=mesh['x'=4,'yh'=4,'yl'=2,'zh'=2,'zl'=6,'core'=2] {'yh','yl'}, dimensions={0} | all-to-all | bytes 819200 | tf_op jit(solution)/shard_map/all_to_all | solution.py:249
  85.0 0.6 terms_send.1
  85.6 8.0 %collective-permute-start.1 = (bf16[8,160,128]{2,1,0:T(8,128)(2,1)S(1)}, bf16[8,160,128]{2,1,0:T(8,128)(2,1)S(1)}, u32[]{:S(2)}, u32[]{:S(2)}) collective-permute-start(bf16[8,160,128]{2,1,0:T(8,128)(2,1)S(1)} %terms_send.1), channel_id=1, source_target_pairs={{0,1},{1,0},{2,3},{3,2},{4,5},{5,4},{6,7},{7,6},{8,9},{9,8},{10,11... | collective-permute-start | bytes 983048 | tf_op jit(solution)/shard_map/ppermute | solution.py:277
  93.6 0.6 terms_keep.1.keep_ref
  94.2 0.7 collective-permute-done.1.got_ref
  94.8 0.8 pair.1
  95.6 3.4 %all-to-all-start.3 = ((bf16[8,160,128]{2,1,0:T(8,128)(2,1)}), bf16[8,160,128]{2,1,0:T(8,128)(2,1)S(1)}, u32[]{:S(2)}, u32[]{:S(2)}) async-start(bf16[8,160,128]{2,1,0:T(8,128)(2,1)} %pair.1), calls=%async_computation.3 | async-start | bytes 655360 | tf_op jit(solution)/shard_map/all_to_all | solution.py:249
  99.0 1.0 grads.1
  100.1 0.0 copy-start
  100.1 1.1 copy-done
  101.1 5.6 %all-to-all-done.3.got_ref = bf16[8,160,128]{2,1,0:T(8,128)(2,1)S(1)} async-done(((bf16[8,160,128]{2,1,0:T(8,128)(2,1)}), bf16[8,160,128]{2,1,0:T(8,128)(2,1)S(1)}, u32[]{:S(2)}, u32[]{:S(2)}) %all-to-all-start.3) | async-done | bytes 327712 | tf_op jit(solution)/shard_map/all_to_all | solution.py:249
  106.7 3.6 %all-to-all-start.4 = ((bf16[8,640,128]{2,1,0:T(8,128)(2,1)}), bf16[8,640,128]{2,1,0:T(8,128)(2,1)S(1)}, u32[]{:S(2)}, u32[]{:S(2)}) async-start(bf16[8,640,128]{2,1,0:T(8,128)(2,1)} %copy-done), calls=%async_computation.4 | async-start | bytes 2621440 | tf_op jit(solution)/shard_map/all_to_all | solution.py:249
  110.3 26.4 %all-gather = bf16[1920,128]{1,0:T(8,128)(2,1)S(1)} all-gather(bf16[160,128]{1,0:T(8,128)(2,1)S(1)} %home.1), channel_id=2, replica_groups=mesh['x'=4,'yh'=4,'yl'=2,'zh'=2,'zl'=6,'core'=2] {'zl','core'}, dimensions={0}, use_global_device_ids=true | all-gather | bytes 532480 | tf_op jit(solution)/shard_map/all_gather | solution.py:286
  136.7 0.7 reduce.1
  137.4 0.0 all-to-all-done.4.got_ref
  137.4 1.4 unpack.1
  (1 shorter events, 0.0 us)
Async XLA Ops:
  52.9 17.1 %collective-permute-start = (bf16[2,40,640]{2,1,0:T(8,128)(2,1)S(1)}, bf16[2,40,640]{2,1,0:T(8,128)(2,1)S(1)}, u32[]{:S(2)}, u32[]{:S(2)}) collective-permute-start(bf16[2,40,640]{2,1,0:T(8,128)(2,1)S(1)} %get-tuple-element.10), channel_id=1, source_target_pairs={{0,12},{12,0},{1,13},{13,1},{2,14},{14,2},{3,15},{15,3},{4,16},{16... | collective-permute-start | bytes 307208 | tf_op jit(solution)/shard_map/ppermute | solution.py:269
  85.6 9.2 %collective-permute-start.1 = (bf16[8,160,128]{2,1,0:T(8,128)(2,1)S(1)}, bf16[8,160,128]{2,1,0:T(8,128)(2,1)S(1)}, u32[]{:S(2)}, u32[]{:S(2)}) collective-permute-start(bf16[8,160,128]{2,1,0:T(8,128)(2,1)S(1)} %terms_send.1), channel_id=1, source_target_pairs={{0,1},{1,0},{2,3},{3,2},{4,5},{5,4},{6,7},{7,6},{8,9},{9,8},{10,11... | collective-permute-start | bytes 983048 | tf_op jit(solution)/shard_map/ppermute | solution.py:277
  95.6 11.1 %all-to-all-start.3 = ((bf16[8,160,128]{2,1,0:T(8,128)(2,1)}), bf16[8,160,128]{2,1,0:T(8,128)(2,1)S(1)}, u32[]{:S(2)}, u32[]{:S(2)}) async-start(bf16[8,160,128]{2,1,0:T(8,128)(2,1)} %pair.1), calls=%async_computation.3 | async-start | bytes 655360 | tf_op jit(solution)/shard_map/all_to_all | solution.py:249
  100.1 1.1 copy-start
  106.7 30.7 %all-to-all-start.4 = ((bf16[8,640,128]{2,1,0:T(8,128)(2,1)}), bf16[8,640,128]{2,1,0:T(8,128)(2,1)S(1)}, u32[]{:S(2)}, u32[]{:S(2)}) async-start(bf16[8,640,128]{2,1,0:T(8,128)(2,1)} %copy-done), calls=%async_computation.4 | async-start | bytes 2621440 | tf_op jit(solution)/shard_map/all_to_all | solution.py:249
